TPU v7x, 128 devices: a whole 4x4x4 slice. The times are simulated.
128 devices in a mesh: dp: 16 (over x, y), tensor: 8 (over z, core).
Axes of the slice: x: 4, y: 4, z: 4, core: 2. Of those that a mesh axis runs over, the one named last changes fastest.
Arguments:
- hidden_in: bfloat16 [6144, 4096], P('dp', 'tensor'), may hold values from -48 to 48
- encodings: bfloat16 [1024, 128, 896], P('dp', 'tensor'), may hold values from -48 to 48
- nbr_shard: int32 [96, 2], P('dp'), may hold values from 0 to 15, all different within a row; in each aligned block of 6 rows (0 to 5, 6 to 11, ...) at most 2 rows name the same one
- nbr_row: int32 [96, 2], P('dp'), may hold values from 0 to 63
- w_query: bfloat16 [4096, 4096], P(None, 'tensor'), may hold values from -0.09375 to 0.09375
- w_key: bfloat16 [896, 4096], P(None, 'tensor'), may hold values from -0.1875 to 0.1875
- w_value: bfloat16 [896, 4096], P(None, 'tensor'), may hold values from -0.1875 to 0.1875
- w_output: bfloat16 [4096, 4096], P('tensor'), may hold values from -0.09375 to 0.09375
- cotangent: bfloat16 [6144, 4096], P('dp', 'tensor'), may hold values from -6 to 6
Outputs:
- layer_out: bfloat16 [6144, 4096], P('dp', 'tensor')
- grad_hidden: bfloat16 [6144, 4096], P('dp', 'tensor')
- grad_encodings: float32 [1024, 128, 896], P('dp', 'tensor')
- grad_query: float32 [4096, 4096], P('dp', 'tensor')
- grad_key: float32 [896, 4096], P('dp', 'tensor')
- grad_value: float32 [896, 4096], P('dp', 'tensor')
- grad_output: float32 [4096, 4096], P('tensor', 'dp')
Inputs may be any that keep to these rules, and one draw needn't show every extreme that they name: `nbr_shard`: in the 6 spans of one index of dp no shard is named more than 2 times, and one is named exactly 2 times in some of them; the 2 shards of a span differ.
All inputs are finite; a program needn't handle non-finite values.
Results may differ from a plain program's by a relative error of at most 0.02.
Values may be sent and summed in bfloat16 or wider, within the bound.
A program may use at most 128 MiB of HBM per device.

v0:
```python
import math

import jax
import jax.numpy as jnp
from jax import lax
from jax.sharding import PartitionSpec as P

HD = 128
SPAN = 64
NB = 128
K_NBR = 2


def shards(hidden_in, encodings, nbr_shard, nbr_row, w_query, w_key, w_value, w_output, cotangent):
    n_shards = lax.axis_size("dp")
    tok_rows = hidden_in.shape[0]
    columns = w_query.shape[1]
    heads_here = columns // HD
    span_count = tok_rows // SPAN
    live_blocks = K_NBR * span_count
    capacity = max(2, 4 * span_count // n_shards)
    slot_count = n_shards * capacity
    db_blocks = encodings.shape[0]
    block_part = encodings.shape[1]
    width = encodings.shape[2]
    scale = 1.0 / math.sqrt(HD)
    owners = nbr_shard.reshape(live_blocks)
    rowids = nbr_row.reshape(live_blocks)
    order = jnp.arange(live_blocks, dtype=jnp.int32)
    earlier = (owners[:, None] == owners[None, :]) & (order[None, :] < order[:, None])
    position = jnp.sum(earlier.astype(jnp.int32), axis=1)
    slot_of = owners * capacity + position
    picked = slot_of[:, None] == jnp.arange(slot_count, dtype=jnp.int32)[None, :]
    request = jnp.sum(jnp.where(picked, rowids[:, None] + 1, 0), axis=0) - 1
    wanted = lax.all_to_all(
        request.reshape(n_shards, capacity), "dp", split_axis=0, concat_axis=0, tiled=True
    )
    table = (
        wanted.reshape(slot_count)[:, None] == jnp.arange(db_blocks, dtype=jnp.int32)[None, :]
    ).astype(jnp.bfloat16)
    outgoing = jnp.dot(
        table, encodings.reshape(db_blocks, block_part * width), preferred_element_type=jnp.float32
    )
    outgoing = outgoing.astype(jnp.bfloat16).reshape(n_shards, capacity, block_part, width)
    arrived = lax.all_to_all(outgoing, "dp", split_axis=0, concat_axis=0, tiled=True).reshape(
        slot_count, block_part, width
    )
    select = picked.astype(jnp.bfloat16)
    gathered = lax.all_gather(arrived, "tensor", axis=1, tiled=True)
    neighbours = jnp.dot(
        select, gathered.reshape(slot_count, NB * width), preferred_element_type=jnp.float32
    )
    neighbours = neighbours.astype(jnp.bfloat16)
    nbr_flat = neighbours.reshape(live_blocks * NB, width)
    hidden_full = lax.all_gather(hidden_in, "tensor", axis=1, tiled=True)
    query = jnp.dot(hidden_full, w_query, preferred_element_type=jnp.float32).astype(jnp.bfloat16)
    keys = jnp.dot(nbr_flat, w_key, preferred_element_type=jnp.float32).astype(jnp.bfloat16)
    values = jnp.dot(nbr_flat, w_value, preferred_element_type=jnp.float32).astype(jnp.bfloat16)
    query_h = query.reshape(span_count, SPAN, heads_here, HD)
    keys_h = keys.reshape(span_count, K_NBR * NB, heads_here, HD)
    values_h = values.reshape(span_count, K_NBR * NB, heads_here, HD)
    scores = (
        jnp.einsum("cqhd,ckhd->chqk", query_h, keys_h, preferred_element_type=jnp.float32) * scale
    )
    probs = jax.nn.softmax(scores, axis=-1)
    probs_b = probs.astype(jnp.bfloat16)
    attended = jnp.einsum("chqk,ckhd->cqhd", probs_b, values_h, preferred_element_type=jnp.float32)
    attended = attended.astype(jnp.bfloat16).reshape(tok_rows, columns)
    out_terms = jnp.dot(attended, w_output, preferred_element_type=jnp.float32)
    layer_out = lax.psum_scatter(out_terms, "tensor", scatter_dimension=1, tiled=True).astype(
        jnp.bfloat16
    )
    grad_full = lax.all_gather(cotangent, "tensor", axis=1, tiled=True)
    grad_att = jnp.dot(grad_full, w_output.T, preferred_element_type=jnp.float32).astype(
        jnp.bfloat16
    )
    grad_output = jnp.dot(attended.T, grad_full, preferred_element_type=jnp.float32)
    grad_att_h = grad_att.reshape(span_count, SPAN, heads_here, HD)
    grad_prob = jnp.einsum(
        "cqhd,ckhd->chqk", grad_att_h, values_h, preferred_element_type=jnp.float32
    )
    inner = jnp.sum(grad_prob * probs, axis=-1, keepdims=True)
    grad_score = (probs * (grad_prob - inner) * scale).astype(jnp.bfloat16)
    grad_v = jnp.einsum("chqk,cqhd->ckhd", probs_b, grad_att_h, preferred_element_type=jnp.float32)
    grad_v = grad_v.astype(jnp.bfloat16).reshape(live_blocks * NB, columns)
    grad_q = jnp.einsum("chqk,ckhd->cqhd", grad_score, keys_h, preferred_element_type=jnp.float32)
    grad_q = grad_q.astype(jnp.bfloat16).reshape(tok_rows, columns)
    grad_k = jnp.einsum("chqk,cqhd->ckhd", grad_score, query_h, preferred_element_type=jnp.float32)
    grad_k = grad_k.astype(jnp.bfloat16).reshape(live_blocks * NB, columns)
    hidden_terms = jnp.dot(grad_q, w_query.T, preferred_element_type=jnp.float32)
    grad_hidden = lax.psum_scatter(hidden_terms, "tensor", scatter_dimension=1, tiled=True).astype(
        jnp.bfloat16
    )
    grad_query = jnp.dot(hidden_full.T, grad_q, preferred_element_type=jnp.float32)
    grad_key = jnp.dot(nbr_flat.T, grad_k, preferred_element_type=jnp.float32)
    grad_value = jnp.dot(nbr_flat.T, grad_v, preferred_element_type=jnp.float32)
    nbr_terms = jnp.dot(grad_k, w_key.T, preferred_element_type=jnp.float32)
    nbr_terms = nbr_terms + jnp.dot(grad_v, w_value.T, preferred_element_type=jnp.float32)
    spread_table = picked.astype(jnp.float32).T
    spread = jnp.dot(
        spread_table, nbr_terms.reshape(live_blocks, NB * width), precision=lax.Precision.HIGHEST
    )
    share = lax.psum_scatter(
        spread.reshape(slot_count, NB, width).astype(jnp.bfloat16),
        "tensor",
        scatter_dimension=1,
        tiled=True,
    ).astype(jnp.float32)
    slot_grad = share.reshape(slot_count, block_part * width)
    returned = lax.all_to_all(
        slot_grad.reshape(n_shards, capacity, block_part, width),
        "dp",
        split_axis=0,
        concat_axis=0,
        tiled=True,
    )
    grad_encodings = jnp.dot(
        table.astype(jnp.float32).T,
        returned.reshape(slot_count, block_part * width),
        precision=lax.Precision.HIGHEST,
    )
    grad_encodings = grad_encodings.reshape(db_blocks, block_part, width)
    summed_q, summed_k, summed_v, summed_o = (
        lax.psum_scatter(
            grad_query.astype(jnp.bfloat16), "dp", scatter_dimension=0, tiled=True
        ).astype(jnp.float32),
        lax.psum_scatter(
            grad_key.astype(jnp.bfloat16), "dp", scatter_dimension=0, tiled=True
        ).astype(jnp.float32),
        lax.psum_scatter(
            grad_value.astype(jnp.bfloat16), "dp", scatter_dimension=0, tiled=True
        ).astype(jnp.float32),
        lax.psum_scatter(
            grad_output.astype(jnp.bfloat16), "dp", scatter_dimension=1, tiled=True
        ).astype(jnp.float32),
    )
    return (layer_out, grad_hidden, grad_encodings, summed_q, summed_k, summed_v, summed_o)


def solution(mesh):
    return jax.shard_map(
        shards,
        mesh=mesh,
        in_specs=(
            P("dp", "tensor"),
            P("dp", "tensor", None),
            P("dp", None),
            P("dp", None),
            P(None, "tensor"),
            P(None, "tensor"),
            P(None, "tensor"),
            P("tensor", None),
            P("dp", "tensor"),
        ),
        out_specs=(
            P("dp", "tensor"),
            P("dp", "tensor"),
            P("dp", "tensor", None),
            P("dp", "tensor"),
            P("dp", "tensor"),
            P("dp", "tensor"),
            P("tensor", "dp"),
        ),
        check_vma=False,
    )
```

profile of v0, /device:TPU:0, one launch (start us, length us, event | category | flops | bytes accessed | tf_op | source)
XLA Modules:
  0.0 686.0 jit_solution(1676179359776295125)
XLA Ops:
  7.2 0.7 all-gather.8.cloned.1.call-update
  8.0 0.7 all-gather.6.cloned.1.call-update
  8.7 0.7 broadcast_add_fusion
  9.5 0.8 copy.67
  10.7 0.7 sub.23
  11.4 7.1 %all-to-all-start = ((s32[16,1,2]{2,1,0:T(1,128)}), s32[16,1,2]{2,1,0:T(1,128)S(1)}, u32[]{:S(2)}, u32[]{:S(2)}) async-start(s32[16,1,2]{2,1,0:T(1,128)} %bitcast), calls=%async_computation | async-start | bytes 16384 | tf_op jit(solution)/shard_map/all_to_all | solution.py:35
  18.5 1.9 copy.89
  20.5 5.5 all-to-all-done
  26.0 0.5 broadcast.55
  26.5 0.7 reduce.3
  27.2 0.5 convolution_convert_fusion.1
  27.8 17.6 %all_to_all.16 = bf16[16,2,16,896]{3,2,1,0:T(8,128)(2,1)} all-to-all(bf16[16,2,16,896]{3,2,1,0:T(8,128)(2,1)S(1)} %bitcast.109), channel_id=1, replica_groups=mesh['dp'=16,'tensor'=8] {'dp'}, dimensions={0} | all-to-all | bytes 1835008 | tf_op jit(solution)/shard_map/all_to_all | solution.py:45
  45.5 5.0 convolution_convert_fusion.8
  50.5 19.2 %all-gather.6.cloned.1.call-done = bf16[384,4096]{1,0:T(8,128)(2,1)} async-done(((bf16[384,512]{1,0:T(8,128)(2,1)}), bf16[384,4096]{1,0:T(8,128)(2,1)}) %all-gather.6.cloned.1.call-update) | async-done | bytes 3145744 | tf_op jit(solution)/shard_map/all_gather | solution.py:55
  69.8 4.9 convolution_convert_fusion.9
  74.8 42.1 %all-gather.4.cloned.1.call-done = bf16[32,128,896]{2,1,0:T(8,128)(2,1)} async-done(((bf16[32,16,896]{2,1,0:T(8,128)(2,1)}), bf16[32,128,896]{2,1,0:T(8,128)(2,1)}) %all-gather.4.cloned.1.call-update) | async-done | bytes 7340048 | tf_op jit(solution)/shard_map/all_gather | solution.py:49
  116.9 7.3 %copy.91 = bf16[4,8,128,896]{3,1,2,0:T(8,128)(2,1)S(1)} copy(bf16[4,8,128,896]{3,2,1,0:T(8,128)(2,1)} %bitcast.102) | data formatting | bytes 14680064
  124.3 3.0 convolution_convert_fusion
  127.3 4.8 reshape.111
  132.1 4.7 convolution_convert_fusion.4
  136.8 2.4 reshape.114
  139.2 4.9 convolution_convert_fusion.5
  144.1 3.5 reshape.112
  147.7 0.7 convolution_multiply_fusion
  148.3 1.4 fusion.95
  150.0 0.8 copy-done.2
  150.9 1.9 fusion.42
  152.8 6.2 fusion.30
  159.0 12.7 %fusion.27 = bf16[6,256,4,128]{1,3,2,0:T(8,128)(2,1)} fusion(f32[6,4,64,256]{3,2,1,0:T(8,128)} %fusion.42, bf16[6,64,4,128]{3,2,1,0:T(4,128)(2,1)S(1)} %reshape.113, f32[6,4,64,256]{3,2,1,0:T(8,128)} %get-tuple-element.36, f32[6,4,64]{2,1,0:T(4,128)S(1)} %get-tuple-element.35), kind=kOutput, calls=%fused_computation.31 | convolution fusion | flops 104204032 | bytes 5117952 | tf_op jit(solution)/shard_map/chqk,cqhd->ckhd/dot_general | solution.py:88
  171.6 3.8 copy.79
  175.4 4.0 copy.81
  179.4 3.4 fusion.17
  182.8 4.2 convolution_add_fusion
  187.0 5.7 reshape.120
  192.7 4.5 copy.96
  197.2 0.4 slice_bitcast_fusion
  197.6 10.6 %fusion.4 = bf16[32,128,896]{2,0,1:T(8,128)(2,1)} fusion(f32[128,896,12]{1,0,2:T(8,128)S(1)} %slice_bitcast_fusion, s32[12]{0:T(128)S(1)} %multiply_add_fusion), kind=kOutput, calls=%fused_computation.6 | convolution fusion | flops 532152704 | bytes 12845104 | tf_op jit(solution)/shard_map/dot_general | solution.py:100
  208.3 4.8 fusion.35
  213.2 4.8 fusion.32
  218.0 0.4 reduce-scatter.20.cloned.1.call-start
  218.4 5.2 fusion.61
  223.6 0.3 copy.73
  224.0 6.3 convolution_convert_fusion.2
  230.4 11.3 %fusion.56 = bf16[6,64,4,128]{3,1,2,0:T(8,128)(2,1)S(1)} fusion(bf16[6,256,4,128]{3,2,1,0:T(4,128)(2,1)S(1)} %reshape.114, f32[6,4,64,256]{3,2,1,0:T(8,128)} %fusion.42, f32[6,4,64,256]{3,2,1,0:T(8,128)} %get-tuple-element.36, f32[6,4,64]{2,1,0:T(4,128)S(1)} %get-tuple-element.35), kind=kOutput, calls=%fused_computation.51 | convolution fusion | flops 103614208 | bytes 5117952 | tf_op jit(solution)/shard_map/chqk,ckhd->cqhd/dot_general | solution.py:86
  241.7 0.3 copy.77
  242.0 6.4 fusion.7
  248.5 6.7 fusion.67
  255.4 6.7 fusion.70
  262.2 2.7 copy.87
  264.9 6.8 all-to-all-start.2
  271.7 73.5 %reduce-scatter.24.cloned.1.call-done = bf16[56,512]{1,0:T(8,128)(2,1)} async-done(((bf16[896,512]{1,0:T(8,128)(2,1)}), bf16[56,512]{1,0:T(8,128)(2,1)}) %reduce-scatter.24.cloned.1.call-update) | async-done | bytes 57360
  345.3 1.5 convert_element_type.118
  346.7 74.1 %reduce-scatter.22.cloned.1.call-done = bf16[56,512]{1,0:T(8,128)(2,1)} async-done(((bf16[896,512]{1,0:T(8,128)(2,1)}), bf16[56,512]{1,0:T(8,128)(2,1)}) %reduce-scatter.22.cloned.1.call-update) | async-done | bytes 57360
  420.8 1.5 convert_element_type.116
  422.3 78.8 %reduce-scatter.20.cloned.1.call-done = bf16[512,256]{1,0:T(8,128)(2,1)} async-done(((bf16[512,4096]{1,0:T(8,128)(2,1)}), bf16[512,256]{1,0:T(8,128)(2,1)}) %reduce-scatter.20.cloned.1.call-update) | async-done | bytes 262160 | tf_op jit(solution)/shard_map/reduce_scatter | solution.py:133
  501.1 1.8 convert_element_type.120
  502.8 78.9 %reduce-scatter.18.cloned.1.call-done = bf16[256,512]{0,1:T(8,128)(2,1)} async-done(((bf16[4096,512]{0,1:T(8,128)(2,1)}), bf16[256,512]{0,1:T(8,128)(2,1)}) %reduce-scatter.18.cloned.1.call-update) | async-done | bytes 262160 | tf_op jit(solution)/shard_map/reduce_scatter | solution.py:124
  581.8 1.9 copy.86
  583.7 42.6 %reduce-scatter.14.cloned.1.call-done = f32[384,512]{1,0:T(8,128)} async-done(((f32[384,4096]{1,0:T(8,128)}), f32[384,512]{1,0:T(8,128)}) %reduce-scatter.14.cloned.1.call-update) | async-done | bytes 786448 | tf_op jit(solution)/shard_map/reduce_scatter | solution.py:91
  626.3 1.9 convert_element_type.106
  628.2 42.6 %reduce-scatter.12.cloned.1.call-done = f32[384,512]{1,0:T(8,128)} async-done(((f32[384,4096]{1,0:T(8,128)}), f32[384,512]{1,0:T(8,128)}) %reduce-scatter.12.cloned.1.call-update) | async-done | bytes 786448 | tf_op jit(solution)/shard_map/reduce_scatter | solution.py:70
  670.8 1.9 convert_element_type.101
  672.7 2.3 fusion.8
  675.0 4.0 copy.85
  (42 shorter events, 1.9 us)
Async XLA Ops:
  7.2 124.9 %copy-start = (bf16[896,512]{1,0:T(8,128)(2,1)S(1)}, bf16[896,512]{1,0:T(8,128)(2,1)}, u32[]{:S(2)}) copy-start(bf16[896,512]{1,0:T(8,128)(2,1)} %param.14) | copy-start | bytes 2752516
  7.2 38.3 %all-gather.8.cloned.1.call-start = ((), (), s32[]{:S(2)}) async-start(), calls=%async_computation.13 | async-start | bytes 3538944 | tf_op jit(solution)/shard_map/all_gather | solution.py:73
  7.9 61.9 %all-gather.6.cloned.1.call-start = ((), (), s32[]{:S(2)}) async-start(), calls=%async_computation.11 | async-start | bytes 3538944 | tf_op jit(solution)/shard_map/all_gather | solution.py:55
  11.4 14.6 %all-to-all-start = ((s32[16,1,2]{2,1,0:T(1,128)}), s32[16,1,2]{2,1,0:T(1,128)S(1)}, u32[]{:S(2)}, u32[]{:S(2)}) async-start(s32[16,1,2]{2,1,0:T(1,128)} %bitcast), calls=%async_computation | async-start | bytes 16384 | tf_op jit(solution)/shard_map/all_to_all | solution.py:35
  18.5 98.4 %all-gather.4.cloned.1.call-start = ((), (), s32[]{:S(2)}) async-start(), calls=%async_computation.10 | async-start | bytes 8257536 | tf_op jit(solution)/shard_map/all_gather | solution.py:49
  45.4 216.8 %reduce-scatter.16.cloned.1.call-start = ((), (), s32[]{:S(2)}) async-start(), calls=%async_computation.15 | async-start | bytes 8257536 | tf_op jit(solution)/shard_map/reduce_scatter | solution.py:103
  148.3 1.7 copy-start.3
  148.3 2.5 copy-start.2
  179.4 3.4 copy-start.4
  179.4 3.4 copy-start.5
  208.3 137.0 %reduce-scatter.24.cloned.1.call-start = ((), (), s32[]{:S(2)}) async-start(), calls=%async_computation.19 | async-start | bytes 974848
  213.1 207.7 %reduce-scatter.22.cloned.1.call-start = ((), (), s32[]{:S(2)}) async-start(), calls=%async_computation.18 | async-start | bytes 974848
  218.0 283.1 %reduce-scatter.20.cloned.1.call-start = ((), (), s32[]{:S(2)}) async-start(), calls=%async_computation.17 | async-start | bytes 4456448 | tf_op jit(solution)/shard_map/reduce_scatter | solution.py:133
  230.3 351.4 %reduce-scatter.18.cloned.1.call-start = ((), (), s32[]{:S(2)}) async-start(), calls=%async_computation.16 | async-start | bytes 4456448 | tf_op jit(solution)/shard_map/reduce_scatter | solution.py:124
  248.4 377.8 %reduce-scatter.14.cloned.1.call-start = ((), (), s32[]{:S(2)}) async-start(), calls=%async_computation.14 | async-start | bytes 7077888 | tf_op jit(solution)/shard_map/reduce_scatter | solution.py:91
  255.2 415.6 %reduce-scatter.12.cloned.1.call-start = ((), (), s32[]{:S(2)}) async-start(), calls=%async_computation.12 | async-start | bytes 7077888 | tf_op jit(solution)/shard_map/reduce_scatter | solution.py:70
  264.9 407.8 %all-to-all-start.2 = ((f32[16,2,16,896]{3,2,1,0:T(8,128)}), f32[16,2,16,896]{3,2,1,0:T(8,128)S(1)}, u32[]{:S(2)}, u32[]{:S(2)}) async-start(f32[16,2,16,896]{3,2,1,0:T(8,128)} %bitcast.104), calls=%async_computation.5 | async-start | bytes 3670016 | tf_op jit(solution)/shard_map/all_to_all | solution.py:110
  675.0 4.0 copy-start.1
Sparse Core Ops, SparseCore 0:
  9.7 30.4 all-gather.7
  41.9 27.8 all-gather.5
  71.5 45.4 all-gather.3
  208.4 47.6 reduce-scatter.15
  259.1 86.0 reduce-scatter.23
  348.6 72.1 reduce-scatter.21
  424.1 76.8 reduce-scatter.19
  504.8 76.9 reduce-scatter.17
  584.2 42.0 reduce-scatter.13
  628.5 42.2 reduce-scatter.11
where the time goes:
time: 695 us; the launch traced here: 686 us
  waiting for transfers between devices  459 us (66%)
  matrix products  117 us (17%)
  local copies, waits for them, and re-layouts  51.2 us (7%)
  blocking collectives  17.6 us (3%)
  starting transfers between devices  14.9 us (2%)
  between operations  14.6 us (2%)
  other arithmetic  11.7 us (2%)
    unnamed x12, waiting for transfers between devices  149 us
    reduce_scatter x1, waiting for transfers between devices, shards(): lax.psum_scatter(grad_query.astype(jnp.bfloat16), 'dp', scatter_dimension...  78.9 us
    reduce_scatter x1, waiting for transfers between devices, shards(): lax.psum_scatter(grad_output.astype(jnp.bfloat16), 'dp', scatter_dimensio...  78.8 us
    reduce_scatter x1, waiting for transfers between devices, shards(): lax.psum_scatter(out_terms, 'tensor', scatter_dimension=1, tiled=True)  42.6 us
    reduce_scatter x1, waiting for transfers between devices, shards(): lax.psum_scatter(hidden_terms, 'tensor', scatter_dimension=1, tiled=True)  42.6 us
    all_gather x1, waiting for transfers between devices, shards(): gathered = lax.all_gather(arrived, 'tensor', axis=1, tiled=True)  42.1 us
    unnamed x19, local copies, waits for them, and re-layouts  21.6 us
    all_gather x1, waiting for transfers between devices, shards(): hidden_full = lax.all_gather(hidden_in, 'tensor', axis=1, tiled=True)  19.2 us
  transfers between devices with their start and end apart: 12, of which 9 were waited for; matrix products, arithmetic and copies ran while one was open for 12% of the time, Pallas kernels for 0%

commit v1 on v0

v1 whole, which is shorter than its diff:
```python
import math

import jax
import jax.numpy as jnp
from jax import lax
from jax.experimental import pallas as pl
from jax.experimental.pallas import tpu as pltpu
from jax.sharding import PartitionSpec as P

HD = 128
SPAN = 64
NB = 128
K_NBR = 2
MESH = pl.DeviceIdType.MESH
BF = jnp.bfloat16
F32 = jnp.float32
ANY = pl.BlockSpec(memory_space=pl.ANY)
VM = pl.BlockSpec(memory_space=pltpu.VMEM)
SM = pl.BlockSpec(memory_space=pltpu.SMEM)
DMA = pltpu.SemaphoreType.DMA
NT = (((1,), (1,)), ((), ()))
TN = (((0,), (0,)), ((), ()))


def mm(a, b):
    return jnp.dot(a, b, preferred_element_type=F32)


def mm_nt(a, b):
    return lax.dot_general(a, b, NT, preferred_element_type=F32)


def mm_tn(a, b):
    return lax.dot_general(a, b, TN, preferred_element_type=F32)


class Place:
    def __init__(self):
        self.d = lax.axis_index("dp")
        self.t = lax.axis_index("tensor")
        self.x, self.y = self.d // 4, self.d % 4
        self.z, self.c = self.t // 2, self.t % 2
        self.partner = self.z * 2 + (1 - self.c)
        self.tr = ((self.z + 1) % 4) * 2 + self.c
        self.tl = ((self.z + 3) % 4) * 2 + self.c
        self.tf = ((self.z + 2) % 4) * 2 + self.c

    def peer(self, n):
        return (self.d + n) % 16

    def source(self, n):
        return (self.d + 16 - n) % 16

    def greet(self):
        barrier = pltpu.get_barrier_semaphore()
        for other in (self.partner, self.tr, self.tl):
            pl.semaphore_signal(barrier, inc=1, device_id=(self.d, other), device_id_type=MESH)

        @pl.loop(1, 16)
        def _(n):
            pl.semaphore_signal(barrier, inc=1, device_id=(self.peer(n), self.t), device_id_type=MESH)

        pl.semaphore_wait(barrier, 18)


def remote(src, dst, send, recv, dev):
    return pltpu.make_async_remote_copy(
        src_ref=src, dst_ref=dst, send_sem=send, recv_sem=recv, device_id=dev, device_id_type=MESH
    )


class Gather:
    def __init__(self, me, buf, half, send, recv):
        self.me, self.buf, self.half, self.send, self.recv = me, buf, half, send, recv

    def copy(self, n, t, dev, part=None):
        view = self.buf.at[t] if part is None else self.buf.at[t, pl.ds(part * self.half, self.half)]
        return remote(view, view, self.send.at[n], self.recv.at[n], (self.me.d, dev))

    def start(self):
        me = self.me
        self.copy(0, me.t, me.tr).start()
        self.copy(1, me.t, me.tl).start()
        self.copy(4, me.t, me.partner).start()

    def forward(self):
        me = self.me
        self.copy(0, me.tl, me.tr).wait_recv()
        self.copy(2, me.tl, me.tr, 0).start()
        self.copy(5, me.tl, me.partner).start()
        self.copy(1, me.tr, me.tl).wait_recv()
        self.copy(3, me.tr, me.tl, 1).start()
        self.copy(6, me.tr, me.partner).start()

    def far(self):
        me = self.me
        self.copy(2, me.tf, me.tr, 0).wait_recv()
        self.copy(3, me.tf, me.tl, 1).wait_recv()
        self.copy(7, me.tf, me.partner).start()

    def other(self, t):
        return t + 1 - 2 * self.me.c

    def pairs(self):
        me = self.me
        for n, t in ((4, me.t), (5, me.tl), (6, me.tr), (7, me.tf)):
            self.copy(n, self.other(t), me.partner).wait_recv()

    def sent(self):
        me = self.me
        self.copy(0, me.t, me.tr).wait_send()
        self.copy(1, me.t, me.tl).wait_send()
        self.copy(2, me.tl, me.tr, 0).wait_send()
        self.copy(3, me.tr, me.tl, 1).wait_send()
        for n, t in ((4, me.t), (5, me.tl), (6, me.tr), (7, me.tf)):
            self.copy(n, t, me.partner).wait_send()


def gather_kernel(
    shard_s, row_s, hid, cot, enc, wq, wo, wk, wv,
    q_o, ga_o, k_o, v_o, h_o, c_o, n_o, want_o,
    H, C, N, encv, outg, arr, req, wanted, want_s, wqv, wov, wkv, wvv, acc,
    load, zs, zr, rs, rr, fs, fr,
):
    me = Place()
    d, t = me.d, me.t
    loads = [
        pltpu.make_async_copy(hid, H.at[t], load.at[0]),
        pltpu.make_async_copy(cot, C.at[t], load.at[1]),
        pltpu.make_async_copy(enc, encv, load.at[2]),
        pltpu.make_async_copy(wq, wqv, load.at[3]),
        pltpu.make_async_copy(wo, wov, load.at[4]),
        pltpu.make_async_copy(wk, wkv, load.at[5]),
        pltpu.make_async_copy(wv, wvv, load.at[6]),
    ]
    for one in loads:
        one.start()
    owners, slots = [], []
    lane = lax.broadcasted_iota(jnp.int32, (8, 128), 1)
    table = jnp.full((8, 128), 0, jnp.int32)
    for k in range(12):
        owner = shard_s[k // 2, k % 2]
        position = jnp.int32(0)
        for other in owners:
            position = position + (other == owner).astype(jnp.int32)
        owners.append(owner)
        slots.append((owner, jnp.minimum(position, 1)))
        table = jnp.where(lane == owner * 2 + position, row_s[k // 2, k % 2], table)
    req[...] = table
    wanted[d] = table
    me.greet()

    def request(n, dst):
        return remote(req, wanted.at[dst], rs.at[n], rr.at[n], (me.peer(n), t))

    @pl.loop(1, 16)
    def _(n):
        request(n, d).start()

    gh = Gather(me, H, 192, zs.at[0], zr.at[0])
    gc = Gather(me, C, 192, zs.at[1], zr.at[1])
    gn = Gather(me, N, 96, zs.at[2], zr.at[2])
    loads[0].wait()
    gh.start()
    loads[1].wait()
    gc.start()
    loads[2].wait()

    @pl.loop(1, 16)
    def _(n):
        request(n, me.source(n)).wait_recv()

    to_s = pltpu.make_async_copy(wanted, want_s, load.at[7])
    to_s.start()
    to_s.wait()

    def fetch(n, dst):
        return remote(outg.at[me.peer(n)], arr.at[dst], fs.at[n], fr.at[n], (me.peer(n), t))

    @pl.loop(1, 16)
    def _(n):
        reader = me.peer(n)
        for p in range(2):
            outg[reader, p] = encv[want_s[reader, 0, d * 2 + p]]
        fetch(n, d).start()

    for p in range(2):
        arr[d, p] = encv[want_s[d, 0, d * 2 + p]]
    gh.forward()

    @pl.loop(1, 16)
    def _(n):
        fetch(n, me.source(n)).wait_recv()

    for k in range(12):
        owner, position = slots[k]
        N[t, k * 16:(k + 1) * 16, :] = arr[owner, position]
    gn.start()
    gc.forward()
    gh.far()
    loads[3].wait()
    gh.pairs()
    h_out = pltpu.make_async_copy(H, h_o, load.at[8])
    h_out.start()
    want_o[...] = wanted[...]
    acc[...] = jnp.zeros_like(acc)

    @pl.loop(0, 8)
    def _(k):
        acc[...] += mm(H[k], wqv[k])

    q_o[...] = acc[...].astype(BF)
    gn.forward()
    gc.far()
    loads[4].wait()
    gc.pairs()
    c_out = pltpu.make_async_copy(C, c_o, load.at[9])
    c_out.start()
    acc[...] = jnp.zeros_like(acc)

    @pl.loop(0, 8)
    def _(k):
        acc[...] += mm_nt(C[k], wov[:, pl.ds(pl.multiple_of(k * 512, 512), 512)])

    ga_o[...] = acc[...].astype(BF)
    gn.far()
    loads[5].wait()
    loads[6].wait()
    gn.pairs()
    n_out = pltpu.make_async_copy(N, n_o, load.at[10])
    n_out.start()

    @pl.loop(0, 8)
    def _(k):
        k_o[k] = mm(N[k], wkv[...]).astype(BF)
        v_o[k] = mm(N[k], wvv[...]).astype(BF)

    gh.sent()
    gc.sent()
    gn.sent()

    @pl.loop(1, 16)
    def _(n):
        request(n, d).wait_send()
        fetch(n, d).wait_send()

    h_out.wait()
    c_out.wait()
    n_out.wait()


def gather_call(nbr_shard, nbr_row, hidden_in, cotangent, encodings, wq, wo, wk, wv):
    S = jax.ShapeDtypeStruct
    return pl.pallas_call(
        gather_kernel,
        name="gather",
        out_shape=(
            S((384, 512), BF), S((384, 512), BF), S((8, 192, 512), BF), S((8, 192, 512), BF),
            S((8, 384, 512), BF), S((8, 384, 512), BF), S((8, 192, 896), BF), S((16, 8, 128), jnp.int32),
        ),
        in_specs=[SM, SM] + [ANY] * 7,
        out_specs=(VM, VM, VM, VM, ANY, ANY, ANY, VM),
        scratch_shapes=[
            pltpu.VMEM((8, 384, 512), BF),
            pltpu.VMEM((8, 384, 512), BF),
            pltpu.VMEM((8, 192, 896), BF),
            pltpu.VMEM((64, 16, 896), BF),
            pltpu.VMEM((16, 2, 16, 896), BF),
            pltpu.VMEM((16, 2, 16, 896), BF),
            pltpu.VMEM((8, 128), jnp.int32),
            pltpu.VMEM((16, 8, 128), jnp.int32),
            pltpu.SMEM((16, 8, 128), jnp.int32),
            pltpu.VMEM((8, 512, 512), BF),
            pltpu.VMEM((512, 4096), BF),
            pltpu.VMEM((896, 512), BF),
            pltpu.VMEM((896, 512), BF),
            pltpu.VMEM((384, 512), F32),
            DMA((11,)), DMA((3, 8)), DMA((3, 8)), DMA((16,)), DMA((16,)), DMA((16,)), DMA((16,)),
        ],
        compiler_params=pltpu.CompilerParams(
            collective_id=1, has_side_effects=True, vmem_limit_bytes=56 * 2**20
        ),
    )(nbr_shard, nbr_row, hidden_in, cotangent, encodings, wq, wo, wk, wv)


def attend_kernel(q_ref, ga_ref, k_ref, v_ref, att_ref, gq_ref, gk_ref, gv_ref):
    scale = 1.0 / math.sqrt(HD)
    for h in range(4):
        cols = slice(h * HD, (h + 1) * HD)
        q, ga = q_ref[:, cols], ga_ref[:, cols]
        k = k_ref[:, :, cols].reshape(256, HD)
        v = v_ref[:, :, cols].reshape(256, HD)
        s = mm_nt(q, k) * scale
        e = jnp.exp(s - jnp.max(s, axis=-1, keepdims=True))
        p = e / jnp.sum(e, axis=-1, keepdims=True)
        pb = p.astype(BF)
        att_ref[:, cols] = mm(pb, v).astype(BF)
        gp = mm_nt(ga, v)
        inner = jnp.sum(gp * p, axis=-1, keepdims=True)
        gs = (p * (gp - inner) * scale).astype(BF)
        gv_ref[:, :, cols] = mm_tn(pb, ga).astype(BF).reshape(8, 32, HD)
        gq_ref[:, cols] = mm(gs, k).astype(BF)
        gk_ref[:, :, cols] = mm_tn(gs, q).astype(BF).reshape(8, 32, HD)


def attend_call(q, ga, k, v):
    S = jax.ShapeDtypeStruct
    tok = pl.BlockSpec((SPAN, 512), lambda i: (i, 0))
    nbr = pl.BlockSpec((8, 32, 512), lambda i: (0, i, 0))
    return pl.pallas_call(
        attend_kernel,
        name="attend",
        grid=(6,),
        out_shape=(S((384, 512), BF), S((384, 512), BF), S((8, 192, 512), BF), S((8, 192, 512), BF)),
        in_specs=[tok, tok, nbr, nbr],
        out_specs=(tok, tok, nbr, nbr),
        compiler_params=pltpu.CompilerParams(vmem_limit_bytes=32 * 2**20),
    )(q, ga, k, v)


class Ring:
    def __init__(self, group, f1, f2, send, recv, pos, right, left):
        self.group, self.f1, self.f2 = group, f1, f2
        self.pos = pos
        self.r1, self.r2, self.l1 = (pos + 1) % 4, (pos + 2) % 4, (pos + 3) % 4

        def cp(n, src, dst, dev):
            return remote(src, dst, send.at[n], recv.at[n], dev)

        self.s = [
            cp(0, group(self.r2, 0), f1.at[0], right),
            cp(1, group(self.r2, 1), f1.at[1], left),
            cp(2, group(self.r1, 1), f2.at[0, 1], right),
            cp(3, group(self.l1, 0), f2.at[1, 0], left),
            cp(4, group(self.r1, 0), f2.at[0, 0], right),
            cp(5, group(self.l1, 1), f2.at[1, 1], left),
        ]

    def first(self):
        self.s[0].start()
        self.s[1].start()

    def second(self):
        self.s[2].start()
        self.s[3].start()

    def middle(self):
        self.s[0].wait_recv()
        add_into(self.group(self.r1, 0), self.f1.at[0])
        self.s[4].start()
        self.s[1].wait_recv()
        add_into(self.group(self.l1, 1), self.f1.at[1])
        self.s[5].start()

    def arrive(self):
        for n in range(2, 6):
            self.s[n].wait_recv()

    def sum_in_place(self):
        for h in range(2):
            add_into(self.group(self.pos, h), self.f2.at[0, h], self.f2.at[1, h])

    def total(self, h):
        return (
            self.group(self.pos, h)[...].astype(F32)
            + self.f2[0, h].astype(F32)
            + self.f2[1, h].astype(F32)
        )

    def sent(self):
        for n in range(6):
            self.s[n].wait_send()


def add_into(dst, *srcs):
    lead, rows = dst.shape[:-2], dst.shape[-2]
    step = 32 if rows % 32 == 0 else 16

    def part(*where):
        value = dst[where].astype(F32)
        for src in srcs:
            value = value + src[where].astype(F32)
        dst[where] = value.astype(BF)

    if lead:

        @pl.loop(0, lead[0])
        def _(q):
            @pl.loop(0, rows // step)
            def _(r):
                part(q, pl.ds(pl.multiple_of(r * step, step), step))
    else:

        @pl.loop(0, rows // step)
        def _(r):
            part(pl.ds(pl.multiple_of(r * step, step), step))


def reduce_kernel(
    shard_s, att, gq, gk, gv, h_i, c_i, n_i, wq, wo, wk, wv,
    out_o, hid_o, ret_o, gq_o, gk_o, gv_o, go_o,
    attv, gqv, attT, gqT, gkv, gvv, H, C, N, W, wkv, wvv, GK, GV,
    Bq, Bo, Ba, Bb, q1, q2, o1, o2, a1, a2, b1, b2, q3, q4, o3, o4, a3, a4, b3, b4,
    T, Uo, Po, Uh, Ph, Tn, Un, Pn, zo1, zo2, zh1, zh2, zn1, zn2, live, spread, ret,
    load, wload, ps, pr, ss, sr, fs, fr,
):
    me = Place()
    d, t, c = me.d, me.t, me.c
    loads = [
        pltpu.make_async_copy(src, dst, load.at[n])
        for n, (src, dst) in enumerate(
            (
                (att, attv), (gq, gqv), (h_i, H), (c_i, C), (gk, gkv), (gv, gvv),
                (wk, wkv), (wv, wvv), (n_i, N),
            )
        )
    ]
    for one in loads:
        one.start()

    right_x = ((me.x + 1) % 4 * 4 + me.y, t)
    left_x = ((me.x + 3) % 4 * 4 + me.y, t)
    right_y = (me.x * 4 + (me.y + 1) % 4, t)
    left_y = (me.x * 4 + (me.y + 3) % 4, t)
    right_z, left_z = (d, me.tr), (d, me.tl)
    along = {"x": (me.x, right_x, left_x), "y": (me.y, right_y, left_y), "z": (me.z, right_z, left_z)}

    def ring(n, group, f1, f2, axis):
        return Ring(group, f1, f2, ss.at[n], sr.at[n], *along[axis])

    def pair(n, buf, f1, f2, f3, f4, first, second):
        mine = along[first][0]
        one = ring(n, lambda g, h: buf.at[g, h], f1, f2, first)
        two = ring(n + 1, lambda g, h: buf.at[mine, g // 2, (g % 2) * 2 + h], f3, f4, second)
        return one, two

    rq, rq2 = pair(0, Bq, q1, q2, q3, q4, "x", "y")
    ro, ro2 = pair(2, Bo, o1, o2, o3, o4, "y", "x")
    ra, ra2 = pair(4, Ba, a1, a2, a3, a4, "x", "y")
    rb, rb2 = pair(6, Bb, b1, b2, b3, b4, "y", "x")
    zo = ring(8, lambda g, h: Uo.at[g, h], zo1, zo2, "z")
    zh = ring(9, lambda g, h: Uh.at[g, h], zh1, zh2, "z")
    zn = ring(10, lambda g, h: Un.at[g, h], zn1, zn2, "z")

    loads[0].wait()
    loads[1].wait()
    attT[...] = attv[...].T
    gqT[...] = gqv[...].T
    live[12] = jnp.zeros((16, 896), BF)
    loads[2].wait()
    loads[3].wait()
    me.greet()

    def weights(group_x, group_y):
        @pl.loop(0, 4)
        def _(s):
            dq = group_x * 4 + s
            do = s * 4 + group_y
            value = mm(gqT[...], H[dq // 2, :, pl.ds(pl.multiple_of((dq % 2) * 256, 256), 256)]).astype(BF)
            Bq[group_x, s // 2, (s % 2) * 2] = value[:256]
            Bq[group_x, s // 2, (s % 2) * 2 + 1] = value[256:]
            value = mm(attT[...], C[do // 2, :, pl.ds(pl.multiple_of((do % 2) * 256, 256), 256)]).astype(BF)
            Bo[group_y, s // 2, (s % 2) * 2] = value[:256]
            Bo[group_y, s // 2, (s % 2) * 2 + 1] = value[256:]

    weights(rq.r2, ro.r2)
    rq.first()
    ro.first()

    def nbr_terms(core, dst):
        @pl.loop(0, 4)
        def _(zz):
            tt = zz * 2 + core
            value = (mm_nt(gkv[tt], wkv[...]) + mm_nt(gvv[tt], wvv[...])).astype(BF)
            dst[zz, 0] = value[:96]
            dst[zz, 1] = value[96:]

    def streamed(left, core, dst, product):
        @pl.loop(0, 4)
        def _(zz):
            value = product(left, zz * 2 + core).astype(BF)
            dst[zz, 0] = value[:192]
            dst[zz, 1] = value[192:]

    def share(n, T, P):
        return remote(T, P, ps.at[n], pr.at[n], (d, me.partner))

    sn, so, sh = share(0, Tn, Pn), share(1, T, Po), share(2, T, Ph)
    for n in range(4, 8):
        loads[n].wait()
    nbr_terms(1 - c, Tn)
    sn.start()
    weights(rq.r1, ro.r1)
    weights(rq.l1, ro.l1)
    rq.second()
    ro.second()
    nbr_terms(c, Un)

    def out_product(left, tt):
        return mm(left[...], W[tt])

    def hid_product(left, tt):
        return mm_nt(left[...], W[tt])

    w_load = [pltpu.make_async_copy(wo.at[:, pl.ds(n * 512, 512)], W.at[n], wload.at[n]) for n in range(8)]
    w_load.append(pltpu.make_async_copy(wq, W, wload.at[8]))
    for n in range(8):
        w_load[n].start()
    sn.wait_recv()

    def merge(U, P):
        @pl.loop(0, 4)
        def _(zz):
            for h in range(2):
                add_into(U.at[zz, h], P.at[zz, h])

    merge(Un, Pn)
    zn.first()
    zn.second()
    for n in range(8):
        w_load[n].wait()
    streamed(attv, 1 - c, T, out_product)
    so.start()
    streamed(attv, c, Uo, out_product)
    w_load[8].start()
    so.wait_recv()
    merge(Uo, Po)
    zo.first()
    zo.second()
    zn.middle()
    rq.middle()
    ro.middle()
    w_load[8].wait()
    so.wait_send()
    streamed(gqv, 1 - c, T, hid_product)
    sh.start()
    streamed(gqv, c, Uh, hid_product)
    sh.wait_recv()
    merge(Uh, Ph)
    zh.first()
    zh.second()
    weights(rq.pos, ro.pos)
    loads[8].wait()

    @pl.loop(0, 7)
    def _(m):
        cols = pl.ds(pl.multiple_of(m * 128, 128), 128)
        left = N[:, :, cols].reshape(1536, 128)
        GK[cols, :] = mm_tn(left, gkv[...].reshape(1536, 512))
        GV[cols, :] = mm_tn(left, gvv[...].reshape(1536, 512))

    @pl.loop(0, 16)
    def _(dd):
        rows = pl.ds(pl.multiple_of(dd * 56, 8), 56)
        value = jnp.concatenate([GK[rows, :], GV[rows, :]], axis=0).astype(BF)
        xx, yy = dd // 4, dd % 4
        Ba[xx, yy // 2, (yy % 2) * 2] = value[:, :128]
        Ba[xx, yy // 2, (yy % 2) * 2 + 1] = value[:, 128:256]
        Bb[yy, xx // 2, (xx % 2) * 2] = value[:, 256:384]
        Bb[yy, xx // 2, (xx % 2) * 2 + 1] = value[:, 384:]

    ra.first()
    rb.first()
    ra.second()
    rb.second()
    zn.arrive()
    for h in range(2):
        value = zn.total(h).astype(BF)
        for k in range(6):
            live[h * 6 + k] = value[k * 16:(k + 1) * 16]
    owners, slots = [], []
    for k in range(12):
        owner = shard_s[k // 2, k % 2]
        position = jnp.int32(0)
        for other in owners:
            position = position + (other == owner).astype(jnp.int32)
        owners.append(owner)
        slots.append(owner * 2 + position)

    def give(n, dst):
        return remote(spread.at[me.peer(n)], ret.at[dst], fs.at[n], fr.at[n], (me.peer(n), t))

    def choose(o, p):
        where = jnp.int32(12)
        for k in range(12):
            where = jnp.where(slots[k] == o * 2 + p, jnp.int32(k), where)
        return where

    @pl.loop(1, 16)
    def _(n):
        o = me.peer(n)
        for p in range(2):
            spread[o, p] = live[choose(o, p)]
        give(n, d).start()

    for p in range(2):
        ret[d, p] = live[choose(d, p)]
    zo.middle()
    zh.middle()
    rq.arrive()
    rq.sum_in_place()
    rq2.first()
    rq2.second()
    ro.arrive()
    ro.sum_in_place()
    ro2.first()
    ro2.second()
    ra.middle()
    rb.middle()
    zo.arrive()
    for h in range(2):
        out_o[h * 192:(h + 1) * 192, :] = zo.total(h).astype(BF)
    zh.arrive()
    for h in range(2):
        hid_o[h * 192:(h + 1) * 192, :] = zh.total(h).astype(BF)
    rq2.middle()
    ro2.middle()
    ra.arrive()
    ra.sum_in_place()
    ra2.first()
    ra2.second()
    rb.arrive()
    rb.sum_in_place()
    rb2.first()
    rb2.second()
    rq2.arrive()
    for h in range(2):
        gq_o[:, h * 256:(h + 1) * 256] = rq2.total(h).T
    ro2.arrive()
    for h in range(2):
        go_o[h * 256:(h + 1) * 256, :] = ro2.total(h)
    ra2.middle()
    rb2.middle()

    @pl.loop(1, 16)
    def _(n):
        give(n, me.source(n)).wait_recv()

    ret_o[...] = ret[...]
    ra2.arrive()
    rb2.arrive()
    for h in range(2):
        for base, one in ((0, ra2), (256, rb2)):
            value = one.total(h)
            low = base + h * 128
            gk_o[:, low:low + 128] = value[:56]
            gv_o[:, low:low + 128] = value[56:]
    for one in (rq, ro, ra, rb, rq2, ro2, ra2, rb2, zo, zh, zn):
        one.sent()
    for one in (sn, sh):
        one.wait_send()

    @pl.loop(1, 16)
    def _(n):
        give(n, d).wait_send()


def reduce_call(nbr_shard, att, gq, gk, gv, h, cc, n, wq, wo, wk, wv):
    S = jax.ShapeDtypeStruct
    V = pltpu.VMEM
    big = [V((4, 2, 4, 256, 256), BF)] * 2 + [V((4, 2, 4, 112, 128), BF)] * 2
    first = []
    for r, w in ((256, 256), (256, 256), (112, 128), (112, 128)):
        first += [V((2, 4, r, w), BF), V((2, 2, 4, r, w), BF)]
    second = []
    for r, w in ((256, 256), (256, 256), (112, 128), (112, 128)):
        second += [V((2, r, w), BF), V((2, 2, r, w), BF)]
    terms = [V((4, 2, 192, 512), BF)] * 5 + [V((4, 2, 96, 896), BF)] * 3
    rings = []
    for r, w in ((192, 512), (192, 512), (96, 896)):
        rings += [V((2, r, w), BF), V((2, 2, r, w), BF)]
    return pl.pallas_call(
        reduce_kernel,
        name="reduce",
        out_shape=(
            S((384, 512), BF), S((384, 512), BF), S((16, 2, 16, 896), BF),
            S((256, 512), F32), S((56, 512), F32), S((56, 512), F32), S((512, 256), F32),
        ),
        in_specs=[SM] + [ANY] * 11,
        out_specs=(VM,) * 7,
        scratch_shapes=[
            V((384, 512), BF), V((384, 512), BF), V((512, 384), BF), V((512, 384), BF),
            V((8, 192, 512), BF), V((8, 192, 512), BF), V((8, 384, 512), BF), V((8, 384, 512), BF),
            V((8, 192, 896), BF), V((8, 512, 512), BF), V((896, 512), BF), V((896, 512), BF),
            V((896, 512), F32), V((896, 512), F32),
        ]
        + big + first + second + terms + rings
        + [
            V((13, 16, 896), BF), V((16, 2, 16, 896), BF), V((16, 2, 16, 896), BF),
            DMA((9,)), DMA((9,)), DMA((3,)), DMA((3,)), DMA((11, 6)), DMA((11, 6)), DMA((16,)), DMA((16,)),
        ],
        compiler_params=pltpu.CompilerParams(
            collective_id=2, has_side_effects=True, vmem_limit_bytes=64 * 2**20 - 2**17
        ),
    )(nbr_shard, att, gq, gk, gv, h, cc, n, wq, wo, wk, wv)


def scatter_kernel(want_s, ret_ref, out_ref):
    out_ref[...] = jnp.zeros_like(out_ref)

    @pl.loop(0, 32)
    def _(s):
        row = want_s[s]
        out_ref[row] += ret_ref[s].astype(F32)


def scatter_call(want, ret):
    return pl.pallas_call(
        scatter_kernel,
        name="scatter",
        out_shape=jax.ShapeDtypeStruct((64, 16, 896), F32),
        in_specs=[SM, VM],
        out_specs=VM,
        compiler_params=pltpu.CompilerParams(vmem_limit_bytes=32 * 2**20),
    )(want, ret)


def shards(hidden_in, encodings, nbr_shard, nbr_row, w_query, w_key, w_value, w_output, cotangent):
    wq = w_query.reshape(8, 512, 512)
    q, ga, k, v, h, c, n, wanted = gather_call(
        nbr_shard, nbr_row, hidden_in, cotangent, encodings, wq, w_output, w_key, w_value
    )
    att, gq, gk, gv = attend_call(q, ga, k, v)
    out, hid, ret, sq, sk, sv, so = reduce_call(
        nbr_shard, att, gq, gk, gv, h, c, n, wq, w_output, w_key, w_value
    )
    d = lax.axis_index("dp")
    want = lax.dynamic_slice(wanted[:, 0, :], (0, d * 2), (16, 2)).reshape(32)
    enc = scatter_call(want, ret.reshape(32, 16, 896))
    return (out, hid, enc, sq, sk, sv, so)


def solution(mesh):
    return jax.shard_map(
        shards,
        mesh=mesh,
        in_specs=(
            P("dp", "tensor"),
            P("dp", "tensor", None),
            P("dp", None),
            P("dp", None),
            P(None, "tensor"),
            P(None, "tensor"),
            P(None, "tensor"),
            P("tensor", None),
            P("dp", "tensor"),
        ),
        out_specs=(
            P("dp", "tensor"),
            P("dp", "tensor"),
            P("dp", "tensor", None),
            P("dp", "tensor"),
            P("dp", "tensor"),
            P("dp", "tensor"),
            P("tensor", "dp"),
        ),
        check_vma=False,
    )
```

time: 695 us -> 172 us (0.25); the launches traced: 686 us -> 172 us
  waiting for transfers between devices: 459 us -> 0 us
  Pallas kernels: 0 us -> 153 us
  matrix products: 117 us -> 0 us
  local copies, waits for them, and re-layouts: 51.2 us -> 17.9 us
  blocking collectives: 17.6 us -> 0 us
  starting transfers between devices: 14.9 us -> 0 us
  between operations: 14.6 us -> 0.73 us
  other arithmetic: 11.7 us -> 0 us
    reduce_scatter x5 -> x0, waiting for transfers between devices: 243 us -> none  [the longest x1 78.9 us: shards(): lax.psum_scatter(grad_query.astype(jnp.bfloat16), 'dp', scatter_dimension...]
    pallas_call x0 -> x4, Pallas kernels: none -> 153 us  [the longest x1 78.4 us: reduce_call(): pl.pallas_call(reduce_kernel, name='reduce', out_shape=(S((384, 512), BF)...]
    unnamed x12 -> x0, waiting for transfers between devices: 149 us -> none
    dot_general x22 -> x0, matrix products: 117 us -> none  [the longest x1 12.7 us: shards(): jnp.einsum('chqk,cqhd->ckhd', grad_score, query_h, preferred_element_type...]
    all_gather x3 -> x0, waiting for transfers between devices: 61.4 us -> none  [the longest x1 42.1 us: shards(): gathered = lax.all_gather(arrived, 'tensor', axis=1, tiled=True)]
    all_to_all x1 -> x0, blocking collectives: 17.6 us -> none  [shards(): lax.all_to_all(outgoing, 'dp', split_axis=0, concat_axis=0, tiled=True)]
    reshape x7 -> x1, local copies, waits for them, and re-layouts: 16.6 us -> 0.08 us  [shards(): want = lax.dynamic_slice(wanted[:, 0, :], (0, d * 2), (16, 2)).reshape(32)]
    all_to_all x2 -> x0, starting transfers between devices: 13.9 us -> none  [the longest x1 7.12 us: shards(): lax.all_to_all(request.reshape(n_shards, capacity), 'dp', split_axis=0, c...]
  transfers between devices with their start and end apart: 12 -> 0, of which waited for: 9 -> 0; matrix products, arithmetic and copies ran while one was open for 12% -> 0% of each run, Pallas kernels for 0% -> 0%
where the time goes in v1:
time: 172 us
  Pallas kernels  153 us (89%)
  local copies, waits for them, and re-layouts  17.9 us (10%)
    pallas_call x1, Pallas kernels, reduce_call(): pl.pallas_call(reduce_kernel, name='reduce', out_shape=(S((384, 512), BF)...  78.4 us
    pallas_call x1, Pallas kernels, gather_call(): pl.pallas_call(gather_kernel, name='gather', out_shape=(S((384, 512), BF)...  59 us
    unnamed x38, local copies, waits for them, and re-layouts  16.9 us
    pallas_call x1, Pallas kernels, attend_call(): pl.pallas_call(attend_kernel, name='attend', grid=(6,), out_shape=(S((384...  12.6 us

profile of v1, /device:TPU:0, one launch (start us, length us, event | category | flops | bytes accessed | tf_op | source)
XLA Modules:
  0.0 171.6 jit_solution(17605701630243268817)
XLA Ops:
  0.6 1.4 copy.21.shard_s
  2.0 1.4 copy.20.row_s
  3.3 59.0 %gather.1 = (bf16[384,512]{1,0:T(8,128)(2,1)}, bf16[384,512]{1,0:T(8,128)(2,1)}, bf16[8,192,512]{2,1,0:T(8,128)(2,1)}, bf16[8,192,512]{2,1,0:T(8,128)(2,1)}, bf1...) custom-call(s32[6,2]{1,0:T(8,128)} %copy.21.shard_s, ...), custom_call_target="tpu_custom_call" | custom-call | tf_op jit(solution)/shard_map/gather/pallas_call | solution.py:254
  62.4 0.0 copy-start.2
  62.4 1.4 copy-done.2
  63.8 0.0 copy-start.3
  63.8 1.4 copy-done.3
  65.2 0.0 copy-start.7
  65.2 1.0 copy-done.7
  66.2 0.0 copy-start.8
  66.2 1.0 copy-done.8
  67.2 12.6 %attend.1 = (bf16[384,512]{1,0:T(8,128)(2,1)S(1)}, bf16[384,512]{1,0:T(8,128)(2,1)S(1)}, bf16[8,192,512]{2,1,0:T(8,128)(2,1)S(1)}, bf16[8,192,512]{2,1,0:T(8,128)(2,1)S(1)}) custom-call(bf16[384,512]{1,0:T(8,128)(2,1)S(1)} %copy-done.7, bf16[384,512]{1,0:T(8,128)(2,1)S(1)} %copy-done.8, bf16[8,192,512]{2,1,0:T(8,128)(2,1)S(1)} %copy-done.2, ...), custom_call_target="tpu_custom_call" | custom-call | tf_op jit(solution)/shard_map/attend/pallas_call | solution.py:310
  79.8 0.0 copy-start
  79.8 1.1 copy-done
  81.0 0.0 copy-start.1
  81.0 1.2 copy-done.1
  82.1 0.0 copy-start.5
  82.1 0.7 copy-done.5
  82.9 0.0 copy-start.6
  82.9 0.7 copy-done.6
  83.6 78.4 %reduce.5 = (bf16[384,512]{1,0:T(8,128)(2,1)}, bf16[384,512]{1,0:T(8,128)(2,1)}, bf16[16,2,16,896]{3,2,1,0:T(8,128)(2,1)}, f32[256,512]{1,0:T(8,128)}, f32[56,51...) custom-call(s32[6,2]{1,0:T(8,128)} %copy.21.shard_s, bf16[384,512]{1,0:T(8,128)(2,1)} %copy-done.5, ...), custom_call_target="tpu_custom_call" | custom-call | tf_op jit(solution)/shard_map/reduce/pallas_call | solution.py:672
  162.0 0.8 slice.3
  162.9 0.1 dynamic-slice_reduce_fusion
  163.0 0.1 reshape.26.want_s
  163.1 0.0 copy-start.4
  163.1 1.2 copy-done.4
  164.3 0.0 copy-start.12
  164.3 0.0 copy-start.11
  164.3 0.0 copy-start.10
  164.3 0.0 copy-start.14
  164.3 0.0 copy-start.13
  164.3 0.0 copy-start.9
  164.3 3.0 %scatter.1 = f32[64,16,896]{2,1,0:T(8,128)} custom-call(s32[32]{0:T(128)S(1)} %reshape.26.want_s, bf16[32,16,896]{2,1,0:T(8,128)(2,1)S(1)} %bitcast.2), custom_call_target="tpu_custom_call" | custom-call | tf_op jit(solution)/shard_map/scatter/pallas_call | solution.py:708
  167.2 0.0 copy-done.12
  167.2 0.7 copy.28
  168.0 0.0 copy-done.11
  168.0 0.7 copy.29
  168.7 0.0 copy-done.10
  168.7 0.8 copy.30
  169.5 0.0 copy-done.14
  169.5 0.6 copy.31
  170.2 0.0 copy-done.13
  170.2 0.6 copy.32
  170.8 0.0 copy-done.9
  170.8 0.8 copy.33
Async XLA Ops:
  62.4 1.4 copy-start.2
  63.8 1.4 copy-start.3
  65.2 1.0 copy-start.7
  66.2 1.0 copy-start.8
  79.8 1.1 copy-start
  81.0 1.2 copy-start.1
  82.1 0.7 copy-start.5
  82.9 0.7 copy-start.6
  163.1 1.2 copy-start.4
  164.3 3.0 %copy-start.12 = (bf16[384,512]{1,0:T(8,128)(2,1)S(1)}, bf16[384,512]{1,0:T(8,128)(2,1)}, u32[]{:S(2)}) copy-start(bf16[384,512]{1,0:T(8,128)(2,1)} %get-tuple-element.52) | copy-start | bytes 1179652
  164.3 3.7 %copy-start.11 = (bf16[384,512]{1,0:T(8,128)(2,1)S(1)}, bf16[384,512]{1,0:T(8,128)(2,1)}, u32[]{:S(2)}) copy-start(bf16[384,512]{1,0:T(8,128)(2,1)} %get-tuple-element.53) | copy-start | bytes 1179652
  164.3 4.5 %copy-start.10 = (f32[256,512]{1,0:T(8,128)S(1)}, f32[256,512]{1,0:T(8,128)}, u32[]{:S(2)}) copy-start(f32[256,512]{1,0:T(8,128)} %get-tuple-element.55) | copy-start | bytes 1572868
  164.3 5.3 %copy-start.14 = (f32[56,512]{1,0:T(8,128)S(1)}, f32[56,512]{1,0:T(8,128)}, u32[]{:S(2)}) copy-start(f32[56,512]{1,0:T(8,128)} %get-tuple-element.56) | copy-start | bytes 344068
  164.3 5.9 %copy-start.13 = (f32[56,512]{1,0:T(8,128)S(1)}, f32[56,512]{1,0:T(8,128)}, u32[]{:S(2)}) copy-start(f32[56,512]{1,0:T(8,128)} %get-tuple-element.57) | copy-start | bytes 344068
  164.3 6.6 %copy-start.9 = (f32[512,256]{1,0:T(8,128)S(1)}, f32[512,256]{1,0:T(8,128)}, u32[]{:S(2)}) copy-start(f32[512,256]{1,0:T(8,128)} %get-tuple-element.58) | copy-start | bytes 1572868

commit v2 on v1

--- a/solution.py
+++ b/solution.py
@@ -101,10 +101,17 @@
     def other(self, t):
         return t + 1 - 2 * self.me.c
 
+    def near_pairs(self):
+        me = self.me
+        for n, t in ((4, me.t), (5, me.tl), (6, me.tr)):
+            self.copy(n, self.other(t), me.partner).wait_recv()
+
+    def last_pair(self):
+        self.copy(7, self.other(self.me.tf), self.me.partner).wait_recv()
+
     def pairs(self):
-        me = self.me
-        for n, t in ((4, me.t), (5, me.tl), (6, me.tr), (7, me.tf)):
-            self.copy(n, self.other(t), me.partner).wait_recv()
+        self.near_pairs()
+        self.last_pair()
 
     def sent(self):
         me = self.me
@@ -116,10 +123,31 @@
             self.copy(n, t, me.partner).wait_send()
 
 
+def attend(q_ref, ga_ref, k_ref, v_ref, att_ref, gq_ref, gk_ref, gv_ref, rows, keys):
+    scale = 1.0 / math.sqrt(HD)
+    heads = [slice(h * HD, (h + 1) * HD) for h in range(4)]
+    q, ga = [q_ref[rows, c] for c in heads], [ga_ref[rows, c] for c in heads]
+    k = [k_ref[:, keys, c].reshape(256, HD) for c in heads]
+    v = [v_ref[:, keys, c].reshape(256, HD) for c in heads]
+    s = [mm_nt(a, b) * scale for a, b in zip(q, k)]
+    gp = [mm_nt(a, b) for a, b in zip(ga, v)]
+    e = [jnp.exp(a - jnp.max(a, axis=-1, keepdims=True)) for a in s]
+    p = [a * (1.0 / jnp.sum(a, axis=-1, keepdims=True)) for a in e]
+    pb = [a.astype(BF) for a in p]
+    inner = [jnp.sum(a * b, axis=-1, keepdims=True) for a, b in zip(gp, p)]
+    gs = [(a * (b - c) * scale).astype(BF) for a, b, c in zip(p, gp, inner)]
+    for n, c in enumerate(heads):
+        att_ref[rows, c] = mm(pb[n], v[n]).astype(BF)
+        gq_ref[rows, c] = mm(gs[n], k[n]).astype(BF)
+    for n, c in enumerate(heads):
+        gv_ref[:, keys, c] = mm_tn(pb[n], ga[n]).astype(BF).reshape(8, 32, HD)
+        gk_ref[:, keys, c] = mm_tn(gs[n], q[n]).astype(BF).reshape(8, 32, HD)
+
+
 def gather_kernel(
     shard_s, row_s, hid, cot, enc, wq, wo, wk, wv,
-    q_o, ga_o, k_o, v_o, h_o, c_o, n_o, want_o,
-    H, C, N, encv, outg, arr, req, wanted, want_s, wqv, wov, wkv, wvv, acc,
+    att_o, gq_o, gk_o, gv_o, h_o, c_o, n_o, want_o,
+    qv, gav, kv, vv, H, C, N, encv, outg, arr, req, wanted, want_s, wqv, wov, wkv, wvv,
     load, zs, zr, rs, rr, fs, fr,
 ):
     me = Place()
@@ -139,13 +167,13 @@
     lane = lax.broadcasted_iota(jnp.int32, (8, 128), 1)
     table = jnp.full((8, 128), 0, jnp.int32)
     for k in range(12):
-        owner = shard_s[k // 2, k % 2]
+        owner = shard_s[k % 2, k // 2]
         position = jnp.int32(0)
         for other in owners:
             position = position + (other == owner).astype(jnp.int32)
         owners.append(owner)
         slots.append((owner, jnp.minimum(position, 1)))
-        table = jnp.where(lane == owner * 2 + position, row_s[k // 2, k % 2], table)
+        table = jnp.where(lane == owner * 2 + position, row_s[k % 2, k // 2], table)
     req[...] = table
     wanted[d] = table
     me.greet()
@@ -198,42 +226,66 @@
     gn.start()
     gc.forward()
     gh.far()
+    for r in range(16):
+        for p in range(2):
+            want_o[r * 2 + p] = want_s[r, 0, d * 2 + p]
     loads[3].wait()
     gh.pairs()
     h_out = pltpu.make_async_copy(H, h_o, load.at[8])
     h_out.start()
-    want_o[...] = wanted[...]
-    acc[...] = jnp.zeros_like(acc)
-
-    @pl.loop(0, 8)
-    def _(k):
-        acc[...] += mm(H[k], wqv[k])
-
-    q_o[...] = acc[...].astype(BF)
+
+    @pl.loop(0, 2)
+    def _(m):
+        cols = pl.ds(pl.multiple_of(m * 256, 256), 256)
+        value = mm(H[0], wqv[0, :, cols])
+        for k in range(1, 8):
+            value = value + mm(H[k], wqv[k, :, cols])
+        qv[:, cols] = value.astype(BF)
+
     gn.forward()
+    loads[4].wait()
+    loads[5].wait()
+    loads[6].wait()
+
+    def project(k):
+        kv[k] = mm(N[k], wkv[...]).astype(BF)
+        vv[k] = mm(N[k], wvv[...]).astype(BF)
+
+    @pl.loop(0, 3)
+    def _(s):
+        project((me.z + (s + 3)) % 4 * 2 + me.c)
+
     gc.far()
-    loads[4].wait()
+    gn.near_pairs()
+
+    @pl.loop(0, 3)
+    def _(s):
+        project((me.z + (s + 3)) % 4 * 2 + 1 - me.c)
+
     gc.pairs()
     c_out = pltpu.make_async_copy(C, c_o, load.at[9])
     c_out.start()
-    acc[...] = jnp.zeros_like(acc)
-
-    @pl.loop(0, 8)
-    def _(k):
-        acc[...] += mm_nt(C[k], wov[:, pl.ds(pl.multiple_of(k * 512, 512), 512)])
-
-    ga_o[...] = acc[...].astype(BF)
     gn.far()
-    loads[5].wait()
-    loads[6].wait()
-    gn.pairs()
+
+    @pl.loop(0, 2)
+    def _(m):
+        cols = pl.ds(pl.multiple_of(m * 256, 256), 256)
+        value = mm_nt(C[0], wov[cols, 0:512])
+        for k in range(1, 8):
+            value = value + mm_nt(C[k], wov[cols, k * 512:(k + 1) * 512])
+        gav[:, cols] = value.astype(BF)
+
+    project(me.tf)
+    gn.last_pair()
     n_out = pltpu.make_async_copy(N, n_o, load.at[10])
     n_out.start()
-
-    @pl.loop(0, 8)
-    def _(k):
-        k_o[k] = mm(N[k], wkv[...]).astype(BF)
-        v_o[k] = mm(N[k], wvv[...]).astype(BF)
+    project((me.z + 2) % 4 * 2 + 1 - me.c)
+
+    @pl.loop(0, 6, unroll=2)
+    def _(s):
+        rows = pl.ds(pl.multiple_of(s * 64, 64), 64)
+        keys = pl.ds(pl.multiple_of(s * 32, 32), 32)
+        attend(qv, gav, kv, vv, att_o, gq_o, gk_o, gv_o, rows, keys)
 
     gh.sent()
     gc.sent()
@@ -256,11 +308,15 @@
         name="gather",
         out_shape=(
             S((384, 512), BF), S((384, 512), BF), S((8, 192, 512), BF), S((8, 192, 512), BF),
-            S((8, 384, 512), BF), S((8, 384, 512), BF), S((8, 192, 896), BF), S((16, 8, 128), jnp.int32),
+            S((8, 384, 512), BF), S((8, 384, 512), BF), S((8, 192, 896), BF), S((32,), jnp.int32),
         ),
         in_specs=[SM, SM] + [ANY] * 7,
-        out_specs=(VM, VM, VM, VM, ANY, ANY, ANY, VM),
+        out_specs=(VM, VM, VM, VM, ANY, ANY, ANY, SM),
         scratch_shapes=[
+            pltpu.VMEM((384, 512), BF),
+            pltpu.VMEM((384, 512), BF),
+            pltpu.VMEM((8, 192, 512), BF),
+            pltpu.VMEM((8, 192, 512), BF),
             pltpu.VMEM((8, 384, 512), BF),
             pltpu.VMEM((8, 384, 512), BF),
             pltpu.VMEM((8, 192, 896), BF),
@@ -274,48 +330,12 @@
             pltpu.VMEM((512, 4096), BF),
             pltpu.VMEM((896, 512), BF),
             pltpu.VMEM((896, 512), BF),
-            pltpu.VMEM((384, 512), F32),
             DMA((11,)), DMA((3, 8)), DMA((3, 8)), DMA((16,)), DMA((16,)), DMA((16,)), DMA((16,)),
         ],
         compiler_params=pltpu.CompilerParams(
             collective_id=1, has_side_effects=True, vmem_limit_bytes=56 * 2**20
         ),
     )(nbr_shard, nbr_row, hidden_in, cotangent, encodings, wq, wo, wk, wv)
-
-
-def attend_kernel(q_ref, ga_ref, k_ref, v_ref, att_ref, gq_ref, gk_ref, gv_ref):
-    scale = 1.0 / math.sqrt(HD)
-    for h in range(4):
-        cols = slice(h * HD, (h + 1) * HD)
-        q, ga = q_ref[:, cols], ga_ref[:, cols]
-        k = k_ref[:, :, cols].reshape(256, HD)
-        v = v_ref[:, :, cols].reshape(256, HD)
-        s = mm_nt(q, k) * scale
-        e = jnp.exp(s - jnp.max(s, axis=-1, keepdims=True))
-        p = e / jnp.sum(e, axis=-1, keepdims=True)
-        pb = p.astype(BF)
-        att_ref[:, cols] = mm(pb, v).astype(BF)
-        gp = mm_nt(ga, v)
-        inner = jnp.sum(gp * p, axis=-1, keepdims=True)
-        gs = (p * (gp - inner) * scale).astype(BF)
-        gv_ref[:, :, cols] = mm_tn(pb, ga).astype(BF).reshape(8, 32, HD)
-        gq_ref[:, cols] = mm(gs, k).astype(BF)
-        gk_ref[:, :, cols] = mm_tn(gs, q).astype(BF).reshape(8, 32, HD)
-
-
-def attend_call(q, ga, k, v):
-    S = jax.ShapeDtypeStruct
-    tok = pl.BlockSpec((SPAN, 512), lambda i: (i, 0))
-    nbr = pl.BlockSpec((8, 32, 512), lambda i: (0, i, 0))
-    return pl.pallas_call(
-        attend_kernel,
-        name="attend",
-        grid=(6,),
-        out_shape=(S((384, 512), BF), S((384, 512), BF), S((8, 192, 512), BF), S((8, 192, 512), BF)),
-        in_specs=[tok, tok, nbr, nbr],
-        out_specs=(tok, tok, nbr, nbr),
-        compiler_params=pltpu.CompilerParams(vmem_limit_bytes=32 * 2**20),
-    )(q, ga, k, v)
 
 
 class Ring:
@@ -570,7 +590,7 @@
             live[h * 6 + k] = value[k * 16:(k + 1) * 16]
     owners, slots = [], []
     for k in range(12):
-        owner = shard_s[k // 2, k % 2]
+        owner = shard_s[k % 2, k // 2]
         position = jnp.int32(0)
         for other in owners:
             position = position + (other == owner).astype(jnp.int32)
@@ -695,38 +715,45 @@
     )(nbr_shard, att, gq, gk, gv, h, cc, n, wq, wo, wk, wv)
 
 
-def scatter_kernel(want_s, ret_ref, out_ref):
+def finish_kernel(want_s, ret, *refs):
+    kept, out_ref, given, sems = refs[:6], refs[6], refs[7:13], refs[13]
+    copies = [pltpu.make_async_copy(a, b, sems.at[n]) for n, (a, b) in enumerate(zip(kept, given))]
+    for one in copies:
+        one.start()
     out_ref[...] = jnp.zeros_like(out_ref)
 
     @pl.loop(0, 32)
     def _(s):
         row = want_s[s]
-        out_ref[row] += ret_ref[s].astype(F32)
-
-
-def scatter_call(want, ret):
+        out_ref[row] += ret[s // 2, s % 2].astype(F32)
+
+    for one in copies:
+        one.wait()
+
+
+def finish_call(want, ret, kept):
+    S = jax.ShapeDtypeStruct
     return pl.pallas_call(
-        scatter_kernel,
-        name="scatter",
-        out_shape=jax.ShapeDtypeStruct((64, 16, 896), F32),
-        in_specs=[SM, VM],
-        out_specs=VM,
-        compiler_params=pltpu.CompilerParams(vmem_limit_bytes=32 * 2**20),
-    )(want, ret)
+        finish_kernel,
+        name="finish",
+        out_shape=(S((64, 16, 896), F32),) + tuple(S(a.shape, a.dtype) for a in kept),
+        in_specs=[SM] + [VM] * 7,
+        out_specs=(VM,) + (ANY,) * 6,
+        scratch_shapes=[DMA((6,))],
+        compiler_params=pltpu.CompilerParams(vmem_limit_bytes=64 * 2**20 - 2**17),
+    )(want, ret, *kept)
 
 
 def shards(hidden_in, encodings, nbr_shard, nbr_row, w_query, w_key, w_value, w_output, cotangent):
     wq = w_query.reshape(8, 512, 512)
-    q, ga, k, v, h, c, n, wanted = gather_call(
-        nbr_shard, nbr_row, hidden_in, cotangent, encodings, wq, w_output, w_key, w_value
+    owners, rows = nbr_shard.T, nbr_row.T
+    att, gq, gk, gv, h, c, n, want = gather_call(
+        owners, rows, hidden_in, cotangent, encodings, wq, w_output, w_key, w_value
     )
-    att, gq, gk, gv = attend_call(q, ga, k, v)
     out, hid, ret, sq, sk, sv, so = reduce_call(
-        nbr_shard, att, gq, gk, gv, h, c, n, wq, w_output, w_key, w_value
+        owners, att, gq, gk, gv, h, c, n, wq, w_output, w_key, w_value
     )
-    d = lax.axis_index("dp")
-    want = lax.dynamic_slice(wanted[:, 0, :], (0, d * 2), (16, 2)).reshape(32)
-    enc = scatter_call(want, ret.reshape(32, 16, 896))
+    enc, out, hid, sq, sk, sv, so = finish_call(want, ret, (out, hid, sq, sk, sv, so))
     return (out, hid, enc, sq, sk, sv, so)
 
 

time: 172 us -> 143 us (0.83)
  local copies, waits for them, and re-layouts: 17.9 us -> 0 us
  Pallas kernels: 153 us -> 142 us
    unnamed x38 -> x0, local copies, waits for them, and re-layouts: 16.9 us -> none
    pallas_call x2 -> x1, Pallas kernels: 15.6 us -> 4.99 us  [finish_call(): pl.pallas_call(finish_kernel, name='finish', out_shape=(S((64, 16, 896),...]
where the time goes in v2:
time: 143 us
  Pallas kernels  142 us (99%)
    pallas_call x1, Pallas kernels, reduce_call(): pl.pallas_call(reduce_kernel, name='reduce', out_shape=(S((384, 512), BF)...  78.6 us
    pallas_call x1, Pallas kernels, gather_call(): pl.pallas_call(gather_kernel, name='gather', out_shape=(S((384, 512), BF)...  58.3 us
    pallas_call x1, Pallas kernels, finish_call(): pl.pallas_call(finish_kernel, name='finish', out_shape=(S((64, 16, 896),...  4.99 us

profile of v2, /device:TPU:0, one launch (start us, length us, event | category | flops | bytes accessed | tf_op | source)
XLA Modules:
  0.0 142.5 jit_solution(818354211233040587)
XLA Ops:
  0.6 58.3 %gather.1 = (bf16[384,512]{1,0:T(8,128)(2,1)}, bf16[384,512]{1,0:T(8,128)(2,1)}, bf16[8,192,512]{2,1,0:T(8,128)(2,1)}, bf16[8,192,512]{2,1,0:T(8,128)(2,1)}, bf1...) custom-call(s32[2,6]{1,0:T(2,128)} %bitcast.5, ...), custom_call_target="tpu_custom_call" | custom-call | tf_op jit(solution)/shard_map/gather/pallas_call | solution.py:306
  58.9 78.6 %reduce.1 = (bf16[384,512]{1,0:T(8,128)(2,1)}, bf16[384,512]{1,0:T(8,128)(2,1)}, bf16[16,2,16,896]{3,2,1,0:T(8,128)(2,1)}, f32[256,512]{1,0:T(8,128)}, f32[56,51...) custom-call(s32[2,6]{1,0:T(2,128)} %bitcast.6, bf16[384,512]{1,0:T(8,128)(2,1)} %get-tuple-element.30.att, ...), custom_call_target="tpu_custom_call" | custom-call | tf_op jit(solution)/shard_map/reduce/pallas_call | solution.py:692
  137.5 5.0 %finish.1 = (f32[64,16,896]{2,1,0:T(8,128)}, bf16[384,512]{1,0:T(8,128)(2,1)}, bf16[384,512]{1,0:T(8,128)(2,1)}, f32[256,512]{1,0:T(8,128)}, f32[56,512]{1,0:T(8...) custom-call(s32[32]{0:T(128)} %get-tuple-element.29.want_s, bf16[16,2,16,896]{3,2,1,0:T(8,128)(2,1)} %get-tuple-element.37.ret, ...), custom_call_target="tpu_custom_call" | custom-call | tf_op jit(solution)/shard_map/finish/pallas_call | solution.py:736

commit v3 on v2

--- a/solution.py
+++ b/solution.py
@@ -144,11 +144,92 @@
         gk_ref[:, keys, c] = mm_tn(gs[n], q[n]).astype(BF).reshape(8, 32, HD)
 
 
-def gather_kernel(
+class Ring:
+    def __init__(self, group, f1, f2, send, recv, pos, right, left):
+        self.group, self.f1, self.f2 = group, f1, f2
+        self.pos = pos
+        self.r1, self.r2, self.l1 = (pos + 1) % 4, (pos + 2) % 4, (pos + 3) % 4
+
+        def cp(n, src, dst, dev):
+            return remote(src, dst, send.at[n], recv.at[n], dev)
+
+        self.s = [
+            cp(0, group(self.r2, 0), f1.at[0], right),
+            cp(1, group(self.r2, 1), f1.at[1], left),
+            cp(2, group(self.r1, 1), f2.at[0, 1], right),
+            cp(3, group(self.l1, 0), f2.at[1, 0], left),
+            cp(4, group(self.r1, 0), f2.at[0, 0], right),
+            cp(5, group(self.l1, 1), f2.at[1, 1], left),
+        ]
+
+    def first(self):
+        self.s[0].start()
+        self.s[1].start()
+
+    def second(self):
+        self.s[2].start()
+        self.s[3].start()
+
+    def middle(self):
+        self.s[0].wait_recv()
+        add_into(self.group(self.r1, 0), self.f1.at[0])
+        self.s[4].start()
+        self.s[1].wait_recv()
+        add_into(self.group(self.l1, 1), self.f1.at[1])
+        self.s[5].start()
+
+    def arrive(self):
+        for n in range(2, 6):
+            self.s[n].wait_recv()
+
+    def sum_in_place(self):
+        for h in range(2):
+            add_into(self.group(self.pos, h), self.f2.at[0, h], self.f2.at[1, h])
+
+    def total(self, h):
+        return (
+            self.group(self.pos, h)[...].astype(F32)
+            + self.f2[0, h].astype(F32)
+            + self.f2[1, h].astype(F32)
+        )
+
+    def sent(self):
+        for n in range(6):
+            self.s[n].wait_send()
+
+
+def add_into(dst, *srcs):
+    lead, rows = dst.shape[:-2], dst.shape[-2]
+    step = 32 if rows % 32 == 0 else 16
+
+    def part(*where):
+        value = dst[where].astype(F32)
+        for src in srcs:
+            value = value + src[where].astype(F32)
+        dst[where] = value.astype(BF)
+
+    if lead:
+
+        @pl.loop(0, lead[0])
+        def _(q):
+            @pl.loop(0, rows // step)
+            def _(r):
+                part(q, pl.ds(pl.multiple_of(r * step, step), step))
+    else:
+
+        @pl.loop(0, rows // step)
+        def _(r):
+            part(pl.ds(pl.multiple_of(r * step, step), step))
+
+
+def layer_kernel(
     shard_s, row_s, hid, cot, enc, wq, wo, wk, wv,
-    att_o, gq_o, gk_o, gv_o, h_o, c_o, n_o, want_o,
+    want_o, out_o, hid_o, ret_o, gq_o, gk_o, gv_o, go_o,
     qv, gav, kv, vv, H, C, N, encv, outg, arr, req, wanted, want_s, wqv, wov, wkv, wvv,
-    load, zs, zr, rs, rr, fs, fr,
+    attv, gqv, gkv, gvv, attT, gqT, GK, GV,
+    Bq, Bo, Ba, Bb, q1, q2, o1, o2, a1, a2, b1, b2, q3, q4, o3, o4, a3, a4, b3, b4,
+    Po, Ph, Pn, zo1, zo2, zh1, zh2, zn1, zn2, ret,
+    load, zs, zr, rs, rr, fs, fr, ps, pr, ss, sr, bs, br,
 ):
     me = Place()
     d, t = me.d, me.t
@@ -231,8 +312,6 @@
             want_o[r * 2 + p] = want_s[r, 0, d * 2 + p]
     loads[3].wait()
     gh.pairs()
-    h_out = pltpu.make_async_copy(H, h_o, load.at[8])
-    h_out.start()
 
     @pl.loop(0, 2)
     def _(m):
@@ -263,8 +342,6 @@
         project((me.z + (s + 3)) % 4 * 2 + 1 - me.c)
 
     gc.pairs()
-    c_out = pltpu.make_async_copy(C, c_o, load.at[9])
-    c_out.start()
     gn.far()
 
     @pl.loop(0, 2)
@@ -277,166 +354,18 @@
 
     project(me.tf)
     gn.last_pair()
-    n_out = pltpu.make_async_copy(N, n_o, load.at[10])
-    n_out.start()
     project((me.z + 2) % 4 * 2 + 1 - me.c)
 
     @pl.loop(0, 6, unroll=2)
     def _(s):
         rows = pl.ds(pl.multiple_of(s * 64, 64), 64)
         keys = pl.ds(pl.multiple_of(s * 32, 32), 32)
-        attend(qv, gav, kv, vv, att_o, gq_o, gk_o, gv_o, rows, keys)
-
-    gh.sent()
-    gc.sent()
-    gn.sent()
+        attend(qv, gav, kv, vv, attv, gqv, gkv, gvv, rows, keys)
 
     @pl.loop(1, 16)
     def _(n):
         request(n, d).wait_send()
         fetch(n, d).wait_send()
-
-    h_out.wait()
-    c_out.wait()
-    n_out.wait()
-
-
-def gather_call(nbr_shard, nbr_row, hidden_in, cotangent, encodings, wq, wo, wk, wv):
-    S = jax.ShapeDtypeStruct
-    return pl.pallas_call(
-        gather_kernel,
-        name="gather",
-        out_shape=(
-            S((384, 512), BF), S((384, 512), BF), S((8, 192, 512), BF), S((8, 192, 512), BF),
-            S((8, 384, 512), BF), S((8, 384, 512), BF), S((8, 192, 896), BF), S((32,), jnp.int32),
-        ),
-        in_specs=[SM, SM] + [ANY] * 7,
-        out_specs=(VM, VM, VM, VM, ANY, ANY, ANY, SM),
-        scratch_shapes=[
-            pltpu.VMEM((384, 512), BF),
-            pltpu.VMEM((384, 512), BF),
-            pltpu.VMEM((8, 192, 512), BF),
-            pltpu.VMEM((8, 192, 512), BF),
-            pltpu.VMEM((8, 384, 512), BF),
-            pltpu.VMEM((8, 384, 512), BF),
-            pltpu.VMEM((8, 192, 896), BF),
-            pltpu.VMEM((64, 16, 896), BF),
-            pltpu.VMEM((16, 2, 16, 896), BF),
-            pltpu.VMEM((16, 2, 16, 896), BF),
-            pltpu.VMEM((8, 128), jnp.int32),
-            pltpu.VMEM((16, 8, 128), jnp.int32),
-            pltpu.SMEM((16, 8, 128), jnp.int32),
-            pltpu.VMEM((8, 512, 512), BF),
-            pltpu.VMEM((512, 4096), BF),
-            pltpu.VMEM((896, 512), BF),
-            pltpu.VMEM((896, 512), BF),
-            DMA((11,)), DMA((3, 8)), DMA((3, 8)), DMA((16,)), DMA((16,)), DMA((16,)), DMA((16,)),
-        ],
-        compiler_params=pltpu.CompilerParams(
-            collective_id=1, has_side_effects=True, vmem_limit_bytes=56 * 2**20
-        ),
-    )(nbr_shard, nbr_row, hidden_in, cotangent, encodings, wq, wo, wk, wv)
-
-
-class Ring:
-    def __init__(self, group, f1, f2, send, recv, pos, right, left):
-        self.group, self.f1, self.f2 = group, f1, f2
-        self.pos = pos
-        self.r1, self.r2, self.l1 = (pos + 1) % 4, (pos + 2) % 4, (pos + 3) % 4
-
-        def cp(n, src, dst, dev):
-            return remote(src, dst, send.at[n], recv.at[n], dev)
-
-        self.s = [
-            cp(0, group(self.r2, 0), f1.at[0], right),
-            cp(1, group(self.r2, 1), f1.at[1], left),
-            cp(2, group(self.r1, 1), f2.at[0, 1], right),
-            cp(3, group(self.l1, 0), f2.at[1, 0], left),
-            cp(4, group(self.r1, 0), f2.at[0, 0], right),
-            cp(5, group(self.l1, 1), f2.at[1, 1], left),
-        ]
-
-    def first(self):
-        self.s[0].start()
-        self.s[1].start()
-
-    def second(self):
-        self.s[2].start()
-        self.s[3].start()
-
-    def middle(self):
-        self.s[0].wait_recv()
-        add_into(self.group(self.r1, 0), self.f1.at[0])
-        self.s[4].start()
-        self.s[1].wait_recv()
-        add_into(self.group(self.l1, 1), self.f1.at[1])
-        self.s[5].start()
-
-    def arrive(self):
-        for n in range(2, 6):
-            self.s[n].wait_recv()
-
-    def sum_in_place(self):
-        for h in range(2):
-            add_into(self.group(self.pos, h), self.f2.at[0, h], self.f2.at[1, h])
-
-    def total(self, h):
-        return (
-            self.group(self.pos, h)[...].astype(F32)
-            + self.f2[0, h].astype(F32)
-            + self.f2[1, h].astype(F32)
-        )
-
-    def sent(self):
-        for n in range(6):
-            self.s[n].wait_send()
-
-
-def add_into(dst, *srcs):
-    lead, rows = dst.shape[:-2], dst.shape[-2]
-    step = 32 if rows % 32 == 0 else 16
-
-    def part(*where):
-        value = dst[where].astype(F32)
-        for src in srcs:
-            value = value + src[where].astype(F32)
-        dst[where] = value.astype(BF)
-
-    if lead:
-
-        @pl.loop(0, lead[0])
-        def _(q):
-            @pl.loop(0, rows // step)
-            def _(r):
-                part(q, pl.ds(pl.multiple_of(r * step, step), step))
-    else:
-
-        @pl.loop(0, rows // step)
-        def _(r):
-            part(pl.ds(pl.multiple_of(r * step, step), step))
-
-
-def reduce_kernel(
-    shard_s, att, gq, gk, gv, h_i, c_i, n_i, wq, wo, wk, wv,
-    out_o, hid_o, ret_o, gq_o, gk_o, gv_o, go_o,
-    attv, gqv, attT, gqT, gkv, gvv, H, C, N, W, wkv, wvv, GK, GV,
-    Bq, Bo, Ba, Bb, q1, q2, o1, o2, a1, a2, b1, b2, q3, q4, o3, o4, a3, a4, b3, b4,
-    T, Uo, Po, Uh, Ph, Tn, Un, Pn, zo1, zo2, zh1, zh2, zn1, zn2, live, spread, ret,
-    load, wload, ps, pr, ss, sr, fs, fr,
-):
-    me = Place()
-    d, t, c = me.d, me.t, me.c
-    loads = [
-        pltpu.make_async_copy(src, dst, load.at[n])
-        for n, (src, dst) in enumerate(
-            (
-                (att, attv), (gq, gqv), (h_i, H), (c_i, C), (gk, gkv), (gv, gvv),
-                (wk, wkv), (wv, wvv), (n_i, N),
-            )
-        )
-    ]
-    for one in loads:
-        one.start()
 
     right_x = ((me.x + 1) % 4 * 4 + me.y, t)
     left_x = ((me.x + 3) % 4 * 4 + me.y, t)
@@ -458,18 +387,12 @@
     ro, ro2 = pair(2, Bo, o1, o2, o3, o4, "y", "x")
     ra, ra2 = pair(4, Ba, a1, a2, a3, a4, "x", "y")
     rb, rb2 = pair(6, Bb, b1, b2, b3, b4, "y", "x")
-    zo = ring(8, lambda g, h: Uo.at[g, h], zo1, zo2, "z")
-    zh = ring(9, lambda g, h: Uh.at[g, h], zh1, zh2, "z")
-    zn = ring(10, lambda g, h: Un.at[g, h], zn1, zn2, "z")
-
-    loads[0].wait()
-    loads[1].wait()
+    zo = ring(8, lambda g, h: H.at[g, pl.ds(h * 192, 192)], zo1, zo2, "z")
+    zh = ring(9, lambda g, h: H.at[4 + g, pl.ds(h * 192, 192)], zh1, zh2, "z")
+    zn = ring(10, lambda g, h: N.at[4 + g, pl.ds(h * 96, 96)], zn1, zn2, "z")
+
     attT[...] = attv[...].T
     gqT[...] = gqv[...].T
-    live[12] = jnp.zeros((16, 896), BF)
-    loads[2].wait()
-    loads[3].wait()
-    me.greet()
 
     def weights(group_x, group_y):
         @pl.loop(0, 4)
@@ -486,135 +409,108 @@
     weights(rq.r2, ro.r2)
     rq.first()
     ro.first()
-
-    def nbr_terms(core, dst):
-        @pl.loop(0, 4)
-        def _(zz):
-            tt = zz * 2 + core
-            value = (mm_nt(gkv[tt], wkv[...]) + mm_nt(gvv[tt], wvv[...])).astype(BF)
-            dst[zz, 0] = value[:96]
-            dst[zz, 1] = value[96:]
-
-    def streamed(left, core, dst, product):
-        @pl.loop(0, 4)
-        def _(zz):
-            value = product(left, zz * 2 + core).astype(BF)
-            dst[zz, 0] = value[:192]
-            dst[zz, 1] = value[192:]
-
-    def share(n, T, P):
-        return remote(T, P, ps.at[n], pr.at[n], (d, me.partner))
-
-    sn, so, sh = share(0, Tn, Pn), share(1, T, Po), share(2, T, Ph)
-    for n in range(4, 8):
-        loads[n].wait()
-    nbr_terms(1 - c, Tn)
-    sn.start()
     weights(rq.r1, ro.r1)
     weights(rq.l1, ro.l1)
     rq.second()
     ro.second()
-    nbr_terms(c, Un)
-
-    def out_product(left, tt):
-        return mm(left[...], W[tt])
-
-    def hid_product(left, tt):
-        return mm_nt(left[...], W[tt])
-
-    w_load = [pltpu.make_async_copy(wo.at[:, pl.ds(n * 512, 512)], W.at[n], wload.at[n]) for n in range(8)]
-    w_load.append(pltpu.make_async_copy(wq, W, wload.at[8]))
-    for n in range(8):
-        w_load[n].start()
-    sn.wait_recv()
-
-    def merge(U, P):
-        @pl.loop(0, 4)
-        def _(zz):
-            for h in range(2):
-                add_into(U.at[zz, h], P.at[zz, h])
-
-    merge(Un, Pn)
-    zn.first()
-    zn.second()
-    for n in range(8):
-        w_load[n].wait()
-    streamed(attv, 1 - c, T, out_product)
-    so.start()
-    streamed(attv, c, Uo, out_product)
-    w_load[8].start()
-    so.wait_recv()
-    merge(Uo, Po)
-    zo.first()
-    zo.second()
-    zn.middle()
-    rq.middle()
-    ro.middle()
-    w_load[8].wait()
-    so.wait_send()
-    streamed(gqv, 1 - c, T, hid_product)
-    sh.start()
-    streamed(gqv, c, Uh, hid_product)
-    sh.wait_recv()
-    merge(Uh, Ph)
-    zh.first()
-    zh.second()
     weights(rq.pos, ro.pos)
-    loads[8].wait()
-
-    @pl.loop(0, 7)
-    def _(m):
-        cols = pl.ds(pl.multiple_of(m * 128, 128), 128)
-        left = N[:, :, cols].reshape(1536, 128)
-        GK[cols, :] = mm_tn(left, gkv[...].reshape(1536, 512))
-        GV[cols, :] = mm_tn(left, gvv[...].reshape(1536, 512))
-
-    @pl.loop(0, 16)
-    def _(dd):
-        rows = pl.ds(pl.multiple_of(dd * 56, 8), 56)
-        value = jnp.concatenate([GK[rows, :], GV[rows, :]], axis=0).astype(BF)
-        xx, yy = dd // 4, dd % 4
-        Ba[xx, yy // 2, (yy % 2) * 2] = value[:, :128]
-        Ba[xx, yy // 2, (yy % 2) * 2 + 1] = value[:, 128:256]
-        Bb[yy, xx // 2, (xx % 2) * 2] = value[:, 256:384]
-        Bb[yy, xx // 2, (xx % 2) * 2 + 1] = value[:, 384:]
+    for low, B in ((0, Ba), (256, Bb)):
+
+        @pl.loop(0, 7)
+        def _(m):
+            cols = pl.ds(pl.multiple_of(m * 128, 128), 128)
+            left = N[:, :, cols].reshape(1536, 128)
+            GK[cols, :] = mm_tn(left, gkv[:, :, low:low + 256].reshape(1536, 256))
+            GV[cols, :] = mm_tn(left, gvv[:, :, low:low + 256].reshape(1536, 256))
+
+        @pl.loop(0, 16)
+        def _(dd):
+            rows = pl.ds(pl.multiple_of(dd * 56, 8), 56)
+            value = jnp.concatenate([GK[rows, :], GV[rows, :]], axis=0).astype(BF)
+            one, two = (dd // 4, dd % 4) if low == 0 else (dd % 4, dd // 4)
+            B[one, two // 2, (two % 2) * 2] = value[:, :128]
+            B[one, two // 2, (two % 2) * 2 + 1] = value[:, 128:]
 
     ra.first()
     rb.first()
     ra.second()
     rb.second()
+    gn.sent()
+
+    def terms(buf, base, core, product):
+        @pl.loop(0, 4)
+        def _(zz):
+            buf[base + zz] = product(zz * 2 + core).astype(BF)
+
+    def nbr_product(tt):
+        return mm_nt(gkv[tt], wkv[...]) + mm_nt(gvv[tt], wvv[...])
+
+    def out_product(tt):
+        return mm(attv[...], wov[:, pl.ds(pl.multiple_of(tt * 512, 512), 512)])
+
+    def hid_product(tt):
+        return mm_nt(gqv[...], wqv[tt])
+
+    def share(n, buf, base, P):
+        return remote(buf.at[pl.ds(base, 4)], P, ps.at[n], pr.at[n], (d, me.partner))
+
+    sn, so, sh = share(0, N, 0, Pn), share(1, C, 0, Po), share(2, C, 4, Ph)
+
+    def merge(buf, base, P):
+        @pl.loop(0, 4)
+        def _(zz):
+            add_into(buf.at[base + zz], P.at[zz])
+
+    terms(N, 0, 1 - me.c, nbr_product)
+    sn.start()
+    terms(N, 4, me.c, nbr_product)
+    sn.wait_recv()
+    merge(N, 4, Pn)
+    zn.first()
+    zn.second()
+    gh.sent()
+    gc.sent()
+    terms(C, 0, 1 - me.c, out_product)
+    so.start()
+    terms(H, 0, me.c, out_product)
+    so.wait_recv()
+    merge(H, 0, Po)
+    zo.first()
+    zo.second()
+    rq.middle()
+    ro.middle()
+    zn.middle()
+    terms(C, 4, 1 - me.c, hid_product)
+    sh.start()
+    terms(H, 4, me.c, hid_product)
+    sh.wait_recv()
+    merge(H, 4, Ph)
+    zh.first()
+    zh.second()
     zn.arrive()
     for h in range(2):
         value = zn.total(h).astype(BF)
         for k in range(6):
-            live[h * 6 + k] = value[k * 16:(k + 1) * 16]
-    owners, slots = [], []
-    for k in range(12):
-        owner = shard_s[k % 2, k // 2]
-        position = jnp.int32(0)
-        for other in owners:
-            position = position + (other == owner).astype(jnp.int32)
-        owners.append(owner)
-        slots.append(owner * 2 + position)
-
+            encv[32 + h * 6 + k] = value[k * 16:(k + 1) * 16]
+    encv[44] = jnp.zeros((16, 896), BF)
     def give(n, dst):
-        return remote(spread.at[me.peer(n)], ret.at[dst], fs.at[n], fr.at[n], (me.peer(n), t))
+        return remote(encv.at[pl.ds(me.peer(n) * 2, 2)], ret.at[dst], bs.at[n], br.at[n], (me.peer(n), t))
 
     def choose(o, p):
         where = jnp.int32(12)
         for k in range(12):
-            where = jnp.where(slots[k] == o * 2 + p, jnp.int32(k), where)
+            where = jnp.where(slots[k][0] * 2 + slots[k][1] == o * 2 + p, jnp.int32(k), where)
         return where
 
     @pl.loop(1, 16)
     def _(n):
         o = me.peer(n)
         for p in range(2):
-            spread[o, p] = live[choose(o, p)]
+            encv[o * 2 + p] = encv[32 + choose(o, p)]
         give(n, d).start()
 
     for p in range(2):
-        ret[d, p] = live[choose(d, p)]
+        ret[d, p] = encv[32 + choose(d, p)]
     zo.middle()
     zh.middle()
     rq.arrive()
@@ -656,7 +552,8 @@
     def _(n):
         give(n, me.source(n)).wait_recv()
 
-    ret_o[...] = ret[...]
+    back = pltpu.make_async_copy(ret, ret_o, load.at[8])
+    back.start()
     ra2.arrive()
     rb2.arrive()
     for h in range(2):
@@ -667,7 +564,8 @@
             gv_o[:, low:low + 128] = value[56:]
     for one in (rq, ro, ra, rb, rq2, ro2, ra2, rb2, zo, zh, zn):
         one.sent()
-    for one in (sn, sh):
+    back.wait()
+    for one in (sn, so, sh):
         one.wait_send()
 
     @pl.loop(1, 16)
@@ -675,44 +573,47 @@
         give(n, d).wait_send()
 
 
-def reduce_call(nbr_shard, att, gq, gk, gv, h, cc, n, wq, wo, wk, wv):
+def layer_call(nbr_shard, nbr_row, hidden_in, cotangent, encodings, wq, wo, wk, wv):
     S = jax.ShapeDtypeStruct
     V = pltpu.VMEM
-    big = [V((4, 2, 4, 256, 256), BF)] * 2 + [V((4, 2, 4, 112, 128), BF)] * 2
-    first = []
-    for r, w in ((256, 256), (256, 256), (112, 128), (112, 128)):
+    tok, nbr, wide = V((384, 512), BF), V((8, 192, 512), BF), V((512, 384), BF)
+    sizes = ((256, 256), (256, 256), (112, 128), (112, 128))
+    big = [V((4, 2, 4, r, w), BF) for r, w in sizes]
+    first, second, rings = [], [], []
+    for r, w in sizes:
         first += [V((2, 4, r, w), BF), V((2, 2, 4, r, w), BF)]
-    second = []
-    for r, w in ((256, 256), (256, 256), (112, 128), (112, 128)):
         second += [V((2, r, w), BF), V((2, 2, r, w), BF)]
-    terms = [V((4, 2, 192, 512), BF)] * 5 + [V((4, 2, 96, 896), BF)] * 3
-    rings = []
     for r, w in ((192, 512), (192, 512), (96, 896)):
         rings += [V((2, r, w), BF), V((2, 2, r, w), BF)]
     return pl.pallas_call(
-        reduce_kernel,
-        name="reduce",
+        layer_kernel,
+        name="layer",
         out_shape=(
-            S((384, 512), BF), S((384, 512), BF), S((16, 2, 16, 896), BF),
+            S((32,), jnp.int32), S((384, 512), BF), S((384, 512), BF), S((16, 2, 16, 896), BF),
             S((256, 512), F32), S((56, 512), F32), S((56, 512), F32), S((512, 256), F32),
         ),
-        in_specs=[SM] + [ANY] * 11,
-        out_specs=(VM,) * 7,
+        in_specs=[SM, SM] + [ANY] * 7,
+        out_specs=(SM, VM, VM, ANY, VM, VM, VM, VM),
         scratch_shapes=[
-            V((384, 512), BF), V((384, 512), BF), V((512, 384), BF), V((512, 384), BF),
-            V((8, 192, 512), BF), V((8, 192, 512), BF), V((8, 384, 512), BF), V((8, 384, 512), BF),
-            V((8, 192, 896), BF), V((8, 512, 512), BF), V((896, 512), BF), V((896, 512), BF),
-            V((896, 512), F32), V((896, 512), F32),
+            tok, tok, nbr, nbr,
+            V((8, 384, 512), BF), V((8, 384, 512), BF), V((8, 192, 896), BF),
+            V((64, 16, 896), BF), V((16, 2, 16, 896), BF), V((16, 2, 16, 896), BF),
+            V((8, 128), jnp.int32), V((16, 8, 128), jnp.int32), pltpu.SMEM((16, 8, 128), jnp.int32),
+            V((8, 512, 512), BF), V((512, 4096), BF), V((896, 512), BF), V((896, 512), BF),
+            tok, tok, nbr, nbr, wide, wide, V((896, 256), F32), V((896, 256), F32),
         ]
-        + big + first + second + terms + rings
+        + big + first + second
+        + [V((4, 384, 512), BF), V((4, 384, 512), BF), V((4, 192, 896), BF)]
+        + rings
         + [
-            V((13, 16, 896), BF), V((16, 2, 16, 896), BF), V((16, 2, 16, 896), BF),
-            DMA((9,)), DMA((9,)), DMA((3,)), DMA((3,)), DMA((11, 6)), DMA((11, 6)), DMA((16,)), DMA((16,)),
+            V((16, 2, 16, 896), BF),
+            DMA((9,)), DMA((3, 8)), DMA((3, 8)), DMA((16,)), DMA((16,)), DMA((16,)), DMA((16,)),
+            DMA((3,)), DMA((3,)), DMA((11, 6)), DMA((11, 6)), DMA((16,)), DMA((16,)),
         ],
         compiler_params=pltpu.CompilerParams(
-            collective_id=2, has_side_effects=True, vmem_limit_bytes=64 * 2**20 - 2**17
+            collective_id=1, has_side_effects=True, vmem_limit_bytes=64 * 2**20 - 2**17
         ),
-    )(nbr_shard, att, gq, gk, gv, h, cc, n, wq, wo, wk, wv)
+    )(nbr_shard, nbr_row, hidden_in, cotangent, encodings, wq, wo, wk, wv)
 
 
 def finish_kernel(want_s, ret, *refs):
@@ -747,11 +648,8 @@
 def shards(hidden_in, encodings, nbr_shard, nbr_row, w_query, w_key, w_value, w_output, cotangent):
     wq = w_query.reshape(8, 512, 512)
     owners, rows = nbr_shard.T, nbr_row.T
-    att, gq, gk, gv, h, c, n, want = gather_call(
+    want, out, hid, ret, sq, sk, sv, so = layer_call(
         owners, rows, hidden_in, cotangent, encodings, wq, w_output, w_key, w_value
-    )
-    out, hid, ret, sq, sk, sv, so = reduce_call(
-        owners, att, gq, gk, gv, h, c, n, wq, w_output, w_key, w_value
     )
     enc, out, hid, sq, sk, sv, so = finish_call(want, ret, (out, hid, sq, sk, sv, so))
     return (out, hid, enc, sq, sk, sv, so)

time: 143 us -> 135 us (0.944)
  Pallas kernels: 142 us -> 134 us
    pallas_call x2 -> x1, Pallas kernels: 137 us -> 129 us  [layer_call(): pl.pallas_call(layer_kernel, name='layer', out_shape=(S((32,), jnp.int32)...]
where the time goes in v3:
time: 135 us
  Pallas kernels  134 us (99%)
    pallas_call x1, Pallas kernels, layer_call(): pl.pallas_call(layer_kernel, name='layer', out_shape=(S((32,), jnp.int32)...  129 us
    pallas_call x1, Pallas kernels, finish_call(): pl.pallas_call(finish_kernel, name='finish', out_shape=(S((64, 16, 896),...  4.99 us

profile of v3, /device:TPU:0, one launch (start us, length us, event | category | flops | bytes accessed | tf_op | source)
XLA Modules:
  0.0 135.0 jit_solution(6384040383892597893)
XLA Ops:
  0.6 129.4 %layer.1 = (s32[32]{0:T(128)}, bf16[384,512]{1,0:T(8,128)(2,1)}, bf16[384,512]{1,0:T(8,128)(2,1)}, bf16[16,2,16,896]{3,2,1,0:T(8,128)(2,1)}, f32[256,512]{1,0:T(...) custom-call(s32[2,6]{1,0:T(2,128)} %bitcast.4, s32[2,6]{1,0:T(2,128)} %bitcast.5, ...), custom_call_target="tpu_custom_call" | custom-call | tf_op jit(solution)/shard_map/layer/pallas_call | solution.py:588
  130.0 5.0 %finish.1 = (f32[64,16,896]{2,1,0:T(8,128)}, bf16[384,512]{1,0:T(8,128)(2,1)}, bf16[384,512]{1,0:T(8,128)(2,1)}, f32[256,512]{1,0:T(8,128)}, f32[56,512]{1,0:T(8...) custom-call(s32[32]{0:T(128)} %get-tuple-element.22.want_s, bf16[16,2,16,896]{3,2,1,0:T(8,128)(2,1)} %get-tuple-element.23.ret, ...), custom_call_target="tpu_custom_call" | custom-call | tf_op jit(solution)/shard_map/finish/pallas_call | solution.py:637

commit v4 on v3

--- a/solution.py
+++ b/solution.py
@@ -224,12 +224,13 @@
 
 def layer_kernel(
     shard_s, row_s, hid, cot, enc, wq, wo, wk, wv,
-    want_o, out_o, hid_o, ret_o, gq_o, gk_o, gv_o, go_o,
+    want_o, out_h, hid_h, ret_o, gq_h, gk_h, gv_h, go_h,
+    out_o, hid_o, gq_o, gk_o, gv_o, go_o,
     qv, gav, kv, vv, H, C, N, encv, outg, arr, req, wanted, want_s, wqv, wov, wkv, wvv,
     attv, gqv, gkv, gvv, attT, gqT, GK, GV,
     Bq, Bo, Ba, Bb, q1, q2, o1, o2, a1, a2, b1, b2, q3, q4, o3, o4, a3, a4, b3, b4,
     Po, Ph, Pn, zo1, zo2, zh1, zh2, zn1, zn2, ret,
-    load, zs, zr, rs, rr, fs, fr, ps, pr, ss, sr, bs, br,
+    load, zs, zr, rs, rr, fs, fr, ps, pr, ss, sr, bs, br, keep,
 ):
     me = Place()
     d, t = me.d, me.t
@@ -393,6 +394,13 @@
 
     attT[...] = attv[...].T
     gqT[...] = gqv[...].T
+
+    kept = [
+        pltpu.make_async_copy(a, b, keep.at[n])
+        for n, (a, b) in enumerate(
+            ((out_o, out_h), (hid_o, hid_h), (gq_o, gq_h), (go_o, go_h), (gk_o, gk_h), (gv_o, gv_h))
+        )
+    ]
 
     def weights(group_x, group_y):
         @pl.loop(0, 4)
@@ -523,12 +531,6 @@
     ro2.second()
     ra.middle()
     rb.middle()
-    zo.arrive()
-    for h in range(2):
-        out_o[h * 192:(h + 1) * 192, :] = zo.total(h).astype(BF)
-    zh.arrive()
-    for h in range(2):
-        hid_o[h * 192:(h + 1) * 192, :] = zh.total(h).astype(BF)
     rq2.middle()
     ro2.middle()
     ra.arrive()
@@ -542,11 +544,21 @@
     rq2.arrive()
     for h in range(2):
         gq_o[:, h * 256:(h + 1) * 256] = rq2.total(h).T
+    kept[2].start()
     ro2.arrive()
     for h in range(2):
         go_o[h * 256:(h + 1) * 256, :] = ro2.total(h)
+    kept[3].start()
     ra2.middle()
     rb2.middle()
+    zo.arrive()
+    for h in range(2):
+        out_o[h * 192:(h + 1) * 192, :] = zo.total(h).astype(BF)
+    kept[0].start()
+    zh.arrive()
+    for h in range(2):
+        hid_o[h * 192:(h + 1) * 192, :] = zh.total(h).astype(BF)
+    kept[1].start()
 
     @pl.loop(1, 16)
     def _(n):
@@ -562,9 +574,13 @@
             low = base + h * 128
             gk_o[:, low:low + 128] = value[:56]
             gv_o[:, low:low + 128] = value[56:]
+    kept[4].start()
+    kept[5].start()
     for one in (rq, ro, ra, rb, rq2, ro2, ra2, rb2, zo, zh, zn):
         one.sent()
     back.wait()
+    for one in kept:
+        one.wait()
     for one in (sn, so, sh):
         one.wait_send()
 
@@ -593,8 +609,9 @@
             S((256, 512), F32), S((56, 512), F32), S((56, 512), F32), S((512, 256), F32),
         ),
         in_specs=[SM, SM] + [ANY] * 7,
-        out_specs=(SM, VM, VM, ANY, VM, VM, VM, VM),
+        out_specs=(SM,) + (ANY,) * 7,
         scratch_shapes=[
+            tok, tok, V((256, 512), F32), V((56, 512), F32), V((56, 512), F32), V((512, 256), F32),
             tok, tok, nbr, nbr,
             V((8, 384, 512), BF), V((8, 384, 512), BF), V((8, 192, 896), BF),
             V((64, 16, 896), BF), V((16, 2, 16, 896), BF), V((16, 2, 16, 896), BF),
@@ -608,7 +625,7 @@
         + [
             V((16, 2, 16, 896), BF),
             DMA((9,)), DMA((3, 8)), DMA((3, 8)), DMA((16,)), DMA((16,)), DMA((16,)), DMA((16,)),
-            DMA((3,)), DMA((3,)), DMA((11, 6)), DMA((11, 6)), DMA((16,)), DMA((16,)),
+            DMA((3,)), DMA((3,)), DMA((11, 6)), DMA((11, 6)), DMA((16,)), DMA((16,)), DMA((6,)),
         ],
         compiler_params=pltpu.CompilerParams(
             collective_id=1, has_side_effects=True, vmem_limit_bytes=64 * 2**20 - 2**17
@@ -617,18 +634,32 @@
 
 
 def finish_kernel(want_s, ret, *refs):
-    kept, out_ref, given, sems = refs[:6], refs[6], refs[7:13], refs[13]
-    copies = [pltpu.make_async_copy(a, b, sems.at[n]) for n, (a, b) in enumerate(zip(kept, given))]
-    for one in copies:
+    kept, out_ref, given = refs[:6], refs[6], refs[7:13]
+    retv, held, encv, get, put = refs[13], refs[14:20], refs[20], refs[21], refs[22]
+    arrive = pltpu.make_async_copy(ret, retv, get.at[6])
+    arrive.start()
+    ins = [pltpu.make_async_copy(a, b, get.at[n]) for n, (a, b) in enumerate(zip(kept, held))]
+    outs = [pltpu.make_async_copy(a, b, put.at[n]) for n, (a, b) in enumerate(zip(held, given))]
+    for one in ins:
         one.start()
-    out_ref[...] = jnp.zeros_like(out_ref)
-
-    @pl.loop(0, 32)
+    encv[...] = jnp.zeros_like(encv)
+    arrive.wait()
+
+    @pl.loop(0, 32, unroll=4)
     def _(s):
         row = want_s[s]
-        out_ref[row] += ret[s // 2, s % 2].astype(F32)
-
-    for one in copies:
+        encv[row] += retv[s // 2, s % 2].astype(F32)
+
+    parts = [
+        pltpu.make_async_copy(encv.at[pl.ds(n * 16, 16)], out_ref.at[pl.ds(n * 16, 16)], put.at[6 + n])
+        for n in range(4)
+    ]
+    for one in parts:
+        one.start()
+    for one, two in zip(ins, outs):
+        one.wait()
+        two.start()
+    for one in outs + parts:
         one.wait()
 
 
@@ -638,9 +669,11 @@
         finish_kernel,
         name="finish",
         out_shape=(S((64, 16, 896), F32),) + tuple(S(a.shape, a.dtype) for a in kept),
-        in_specs=[SM] + [VM] * 7,
-        out_specs=(VM,) + (ANY,) * 6,
-        scratch_shapes=[DMA((6,))],
+        in_specs=[SM] + [ANY] * 7,
+        out_specs=(ANY,) * 7,
+        scratch_shapes=[pltpu.VMEM((16, 2, 16, 896), BF)]
+        + [pltpu.VMEM(a.shape, a.dtype) for a in kept]
+        + [pltpu.VMEM((64, 16, 896), F32), DMA((7,)), DMA((10,))],
         compiler_params=pltpu.CompilerParams(vmem_limit_bytes=64 * 2**20 - 2**17),
     )(want, ret, *kept)
 

time: 135 us -> 135 us (level)
  no operation moved by 1% of the time
where the time goes in v4:
time: 135 us
  Pallas kernels  134 us (99%)
    pallas_call x1, Pallas kernels, layer_call(): pl.pallas_call(layer_kernel, name='layer', out_shape=(S((32,), jnp.int32)...  129 us
    pallas_call x1, Pallas kernels, finish_call(): pl.pallas_call(finish_kernel, name='finish', out_shape=(S((64, 16, 896),...  4.8 us

profile of v4, /device:TPU:0, one launch (start us, length us, event | category | flops | bytes accessed | tf_op | source)
XLA Modules:
  0.0 134.6 jit_solution(17736827900399005127)
XLA Ops:
  0.6 129.2 %layer.1 = (s32[32]{0:T(128)}, bf16[384,512]{1,0:T(8,128)(2,1)}, bf16[384,512]{1,0:T(8,128)(2,1)}, bf16[16,2,16,896]{3,2,1,0:T(8,128)(2,1)}, f32[256,512]{1,0:T(...) custom-call(s32[2,6]{1,0:T(2,128)} %bitcast.4, s32[2,6]{1,0:T(2,128)} %bitcast.5, ...), custom_call_target="tpu_custom_call" | custom-call | tf_op jit(solution)/shard_map/layer/pallas_call | solution.py:604
  129.8 4.8 %finish.1 = (f32[64,16,896]{2,1,0:T(8,128)}, bf16[384,512]{1,0:T(8,128)(2,1)}, bf16[384,512]{1,0:T(8,128)(2,1)}, f32[256,512]{1,0:T(8,128)}, f32[56,512]{1,0:T(8...) custom-call(s32[32]{0:T(128)} %get-tuple-element.22.want_s, bf16[16,2,16,896]{3,2,1,0:T(8,128)(2,1)} %get-tuple-element.23.ret, ...), custom_call_target="tpu_custom_call" | custom-call | tf_op jit(solution)/shard_map/finish/pallas_call | solution.py:668

commit v5 on v4

--- a/solution.py
+++ b/solution.py
@@ -495,6 +495,8 @@
     merge(H, 4, Ph)
     zh.first()
     zh.second()
+    ra.middle()
+    rb.middle()
     zn.arrive()
     for h in range(2):
         value = zn.total(h).astype(BF)
@@ -529,8 +531,6 @@
     ro.sum_in_place()
     ro2.first()
     ro2.second()
-    ra.middle()
-    rb.middle()
     rq2.middle()
     ro2.middle()
     ra.arrive()

time: 135 us -> 133 us (0.985)
  Pallas kernels: 134 us -> 132 us
    pallas_call x1, Pallas kernels: 129 us -> 127 us  [layer_call(): pl.pallas_call(layer_kernel, name='layer', out_shape=(S((32,), jnp.int32)...]
where the time goes in v5:
time: 133 us
  Pallas kernels  132 us (99%)
    pallas_call x1, Pallas kernels, layer_call(): pl.pallas_call(layer_kernel, name='layer', out_shape=(S((32,), jnp.int32)...  127 us
    pallas_call x1, Pallas kernels, finish_call(): pl.pallas_call(finish_kernel, name='finish', out_shape=(S((64, 16, 896),...  4.8 us

profile of v5, /device:TPU:0, one launch (start us, length us, event | category | flops | bytes accessed | tf_op | source)
XLA Modules:
  0.0 132.9 jit_solution(9355497975400270362)
XLA Ops:
  0.6 127.4 %layer.1 = (s32[32]{0:T(128)}, bf16[384,512]{1,0:T(8,128)(2,1)}, bf16[384,512]{1,0:T(8,128)(2,1)}, bf16[16,2,16,896]{3,2,1,0:T(8,128)(2,1)}, f32[256,512]{1,0:T(...) custom-call(s32[2,6]{1,0:T(2,128)} %bitcast.4, s32[2,6]{1,0:T(2,128)} %bitcast.5, ...), custom_call_target="tpu_custom_call" | custom-call | tf_op jit(solution)/shard_map/layer/pallas_call | solution.py:604
  128.1 4.8 %finish.1 = (f32[64,16,896]{2,1,0:T(8,128)}, bf16[384,512]{1,0:T(8,128)(2,1)}, bf16[384,512]{1,0:T(8,128)(2,1)}, f32[256,512]{1,0:T(8,128)}, f32[56,512]{1,0:T(8...) custom-call(s32[32]{0:T(128)} %get-tuple-element.22.want_s, bf16[16,2,16,896]{3,2,1,0:T(8,128)(2,1)} %get-tuple-element.23.ret, ...), custom_call_target="tpu_custom_call" | custom-call | tf_op jit(solution)/shard_map/finish/pallas_call | solution.py:668

commit v6 on v5

--- a/solution.py
+++ b/solution.py
@@ -512,6 +512,12 @@
             where = jnp.where(slots[k][0] * 2 + slots[k][1] == o * 2 + p, jnp.int32(k), where)
         return where
 
+    zo.middle()
+    zh.middle()
+    rq.arrive()
+    rq.sum_in_place()
+    rq2.first()
+    rq2.second()
     @pl.loop(1, 16)
     def _(n):
         o = me.peer(n)
@@ -521,12 +527,6 @@
 
     for p in range(2):
         ret[d, p] = encv[32 + choose(d, p)]
-    zo.middle()
-    zh.middle()
-    rq.arrive()
-    rq.sum_in_place()
-    rq2.first()
-    rq2.second()
     ro.arrive()
     ro.sum_in_place()
     ro2.first()

time: 133 us -> 136 us (1.023)
  Pallas kernels: 132 us -> 135 us
    pallas_call x1, Pallas kernels: 127 us -> 131 us  [layer_call(): pl.pallas_call(layer_kernel, name='layer', out_shape=(S((32,), jnp.int32)...]
where the time goes in v6:
time: 136 us
  Pallas kernels  135 us (99%)
    pallas_call x1, Pallas kernels, layer_call(): pl.pallas_call(layer_kernel, name='layer', out_shape=(S((32,), jnp.int32)...  131 us
    pallas_call x1, Pallas kernels, finish_call(): pl.pallas_call(finish_kernel, name='finish', out_shape=(S((64, 16, 896),...  4.8 us

profile of v6, /device:TPU:0, one launch (start us, length us, event | category | flops | bytes accessed | tf_op | source)
XLA Modules:
  0.0 136.1 jit_solution(1983630048902545020)
XLA Ops:
  0.6 130.7 %layer.1 = (s32[32]{0:T(128)}, bf16[384,512]{1,0:T(8,128)(2,1)}, bf16[384,512]{1,0:T(8,128)(2,1)}, bf16[16,2,16,896]{3,2,1,0:T(8,128)(2,1)}, f32[256,512]{1,0:T(...) custom-call(s32[2,6]{1,0:T(2,128)} %bitcast.4, s32[2,6]{1,0:T(2,128)} %bitcast.5, ...), custom_call_target="tpu_custom_call" | custom-call | tf_op jit(solution)/shard_map/layer/pallas_call | solution.py:604
  131.3 4.8 %finish.1 = (f32[64,16,896]{2,1,0:T(8,128)}, bf16[384,512]{1,0:T(8,128)(2,1)}, bf16[384,512]{1,0:T(8,128)(2,1)}, f32[256,512]{1,0:T(8,128)}, f32[56,512]{1,0:T(8...) custom-call(s32[32]{0:T(128)} %get-tuple-element.22.want_s, bf16[16,2,16,896]{3,2,1,0:T(8,128)(2,1)} %get-tuple-element.23.ret, ...), custom_call_target="tpu_custom_call" | custom-call | tf_op jit(solution)/shard_map/finish/pallas_call | solution.py:668
